TPU v7x, 512 devices: a whole 4x8x8 slice. The times are simulated.
512 devices in a mesh: seq: 128 (over y, z, core), head: 4 (over x).
Axes of the slice: x: 4, y: 8, z: 8, core: 2. Of those that a mesh axis runs over, the one named last changes fastest.
Arguments:
- queries: bfloat16 [16384, 2048], P('seq', 'head'), may hold values from -36 to 36
- keys: bfloat16 [16384, 2048], P('seq', 'head'), may hold values from -6 to 6
- values: bfloat16 [16384, 2048], P('seq', 'head'), may hold values from -6 to 6
- rates: float32 [16384, 4], P('seq', 'head'), may hold values from 0.05 to 1
- gate_fast: bfloat16 [4, 512, 256], P('head'), may hold values from -0.25 to 0.25
- up_fast: bfloat16 [4, 512, 256], P('head'), may hold values from -0.25 to 0.25
- down_fast: bfloat16 [4, 512, 256], P('head'), may hold values from -0.375 to 0.375
Outputs:
- mixed: bfloat16 [16384, 2048], P('seq', 'head')
All inputs are finite; a program needn't handle non-finite values.
Results may differ from a plain program's by a relative error of at most 0.02.
Values may be sent and summed in bfloat16 or wider, within the bound.
A program may use at most 64 MiB of HBM per device.

v0:
```python
import jax
import jax.numpy as jnp
from jax import lax
from jax.sharding import PartitionSpec as P


def passed_along(block, axis, distance):
    devices = range(lax.axis_size(axis))
    route = [(i - distance, i) for i in devices if i - distance in devices]
    return lax.ppermute(block, axis, route)


def dot_high(a, b):
    return jnp.dot(a, b, precision=lax.Precision.HIGHEST, preferred_element_type=jnp.float32)


def gradients(xin, yin, rin, w_gate, w_up, w_down):
    h1 = dot_high(xin, w_gate)
    h3 = dot_high(xin, w_up)
    sig = jax.nn.sigmoid(h1)
    s1 = h1 * sig
    gval = s1 * h3
    err = -rin * yin
    g_down = dot_high(err.T, gval)
    dgv = dot_high(err, w_down)
    g_gate = dot_high(xin.T, dgv * h3 * sig * (1.0 + h1 * (1.0 - sig)))
    g_up = dot_high(xin.T, dgv * s1)
    return (g_gate, g_up, g_down)


def update(weight, grad):
    return weight - 0.05 * grad / jnp.sqrt(jnp.mean(grad * grad, axis=1, keepdims=True) + 1e-06)


def apply_fast(qin, w_gate, w_up, w_down):
    hid = jax.nn.silu(dot_high(qin, w_gate)) * dot_high(qin, w_up)
    out = dot_high(hid, w_down.T)
    return (out / jnp.sqrt(jnp.mean(out * out, axis=1, keepdims=True) + 1e-06)).astype(jnp.bfloat16)


def descend(grads, weights):
    g_gate, g_up, g_down = grads
    w_gate, w_up, w_down = weights
    g_gate, g_up, g_down = lax.psum((g_gate, g_up, g_down), "seq")
    return (update(w_gate, g_gate), update(w_up, g_up), update(w_down, g_down))


def local(queries, keys, values, rates, gate_fast, up_fast, down_fast):
    tok_rows, width = queries.shape
    n_seq = lax.axis_size("seq")
    position = lax.axis_index("seq")
    prev_keys, prev_values = passed_along((keys, values), "seq", 1)
    near_keys = jnp.concatenate([prev_keys, keys], axis=0)
    near_values = jnp.concatenate([prev_values, values], axis=0)
    scores = jnp.einsum(
        "td,sd->ts", queries, near_keys, preferred_element_type=jnp.float32
    ) / jnp.sqrt(jnp.float32(width))
    row_pos = jnp.arange(tok_rows)[:, None]
    col_pos = jnp.arange(2 * tok_rows)[None, :]
    valid = (
        (col_pos > row_pos)
        & (col_pos <= row_pos + tok_rows)
        & ((col_pos >= tok_rows) | (position > 0))
    )
    scores = jnp.where(valid, scores, jnp.float32(-1e30))
    top = jnp.max(scores, axis=1, keepdims=True)
    expd = jnp.exp(scores - top)
    probs = (expd / jnp.sum(expd, axis=1, keepdims=True)).astype(jnp.bfloat16)
    attn = jnp.dot(probs, near_values, preferred_element_type=jnp.float32)
    per_peer = tok_rows // n_seq
    half_axis = n_seq // 2
    weights = (
        gate_fast[0].astype(jnp.float32),
        up_fast[0].astype(jnp.float32),
        down_fast[0].astype(jnp.float32),
    )

    def spread(field):
        return field.reshape(per_peer, n_seq, field.shape[1])

    got_q, got_k, got_v, got_r = (
        lax.all_to_all(spread(queries), "seq", split_axis=1, concat_axis=1, tiled=True),
        lax.all_to_all(spread(keys), "seq", split_axis=1, concat_axis=1, tiled=True),
        lax.all_to_all(spread(values), "seq", split_axis=1, concat_axis=1, tiled=True),
        lax.all_to_all(
            spread(rates).astype(jnp.bfloat16), "seq", split_axis=1, concat_axis=1, tiled=True
        ).astype(jnp.float32),
    )

    def span_rows(field, span):
        part = field[:, span * half_axis : (span + 1) * half_axis]
        return part.reshape(per_peer * half_axis, field.shape[2]).astype(jnp.float32)

    outputs = []
    for span in range(2):
        grads = gradients(
            span_rows(got_k, span),
            span_rows(got_v, span),
            span_rows(got_r, span),
            weights[0],
            weights[1],
            weights[2],
        )
        weights = descend(grads, weights)
        fast = apply_fast(span_rows(got_q, span), weights[0], weights[1], weights[2])
        outputs.append(fast.reshape(per_peer, half_axis, width))
    sending = jnp.concatenate(outputs, axis=1)
    back = lax.all_to_all(sending, "seq", split_axis=1, concat_axis=1, tiled=True)
    back = back.reshape(tok_rows, width)
    return (attn + back.astype(jnp.float32)).astype(jnp.bfloat16)


def solution(mesh):
    return jax.shard_map(
        local,
        mesh=mesh,
        in_specs=(
            P("seq", "head"),
            P("seq", "head"),
            P("seq", "head"),
            P("seq", "head"),
            P("head", None, None),
            P("head", None, None),
            P("head", None, None),
        ),
        out_specs=P("seq", "head"),
        check_vma=False,
    )
```

profile of v0, /device:TPU:1, one launch (start us, length us, event | category | flops | bytes accessed | tf_op | source)
XLA Modules:
  0.0 517.3 jit_solution(16254240947207406124)
XLA Ops:
  6.5 0.7 convert_bitcast_fusion
  7.2 0.8 copy.22
  8.0 18.4 %all-to-all-start = ((bf16[1,128,1]{2,0,1:T(2,128)(2,1)}), bf16[1,128,1]{2,0,1:T(2,128)(2,1)S(1)}, u32[]{:S(2)}, u32[]{:S(2)}) async-start(bf16[1,128,1]{2,0,1:T(2,128)(2,1)} %copy.22), calls=%async_computation | async-start | bytes 131072 | tf_op jit(solution)/shard_map/all_to_all | solution.py:85
  27.1 1.3 reduce.4
  28.4 0.7 reshape.170
  29.1 8.8 %all-to-all-done = bf16[1,128,1]{2,0,1:T(2,128)(2,1)S(1)} async-done(((bf16[1,128,1]{2,0,1:T(2,128)(2,1)}), bf16[1,128,1]{2,0,1:T(2,128)(2,1)S(1)}, u32[]{:S(2)}, u32[]{:S(2)}) %all-to-all-start) | async-done | bytes 288 | tf_op jit(solution)/shard_map/all_to_all | solution.py:85
  38.0 5.7 %all-to-all-start.1 = ((bf16[128,2,256]{2,1,0:T(2,128)(2,1)}), bf16[128,2,256]{2,1,0:T(2,128)(2,1)S(1)}, u32[]{:S(2)}, u32[]{:S(2)}) async-start(bf16[128,2,256]{2,1,0:T(2,128)(2,1)} %reshape.170), calls=%async_computation.1 | async-start | bytes 262144 | tf_op jit(solution)/shard_map/all_to_all | solution.py:84
  43.9 1.3 reduce.5
  46.0 10.0 %all-to-all-done.1 = bf16[128,2,256]{2,1,0:T(2,128)(2,1)S(1)} async-done(((bf16[128,2,256]{2,1,0:T(2,128)(2,1)}), bf16[128,2,256]{2,1,0:T(2,128)(2,1)S(1)}, u32[]{:S(2)}, u32[]{:S(2)}) %all-to-all-start.1) | async-done | bytes 131104 | tf_op jit(solution)/shard_map/all_to_all | solution.py:84
  56.0 6.2 %all-to-all-start.2 = ((bf16[128,2,256]{2,1,0:T(2,128)(2,1)}), bf16[128,2,256]{2,1,0:T(2,128)(2,1)S(1)}, u32[]{:S(2)}, u32[]{:S(2)}) async-start(bf16[128,2,256]{2,1,0:T(2,128)(2,1)} %reshape.168), calls=%async_computation.2 | async-start | bytes 262144 | tf_op jit(solution)/shard_map/all_to_all | solution.py:83
  63.4 11.1 %all-to-all-done.2 = bf16[128,2,256]{2,1,0:T(2,128)(2,1)S(1)} async-done(((bf16[128,2,256]{2,1,0:T(2,128)(2,1)}), bf16[128,2,256]{2,1,0:T(2,128)(2,1)S(1)}, u32[]{:S(2)}, u32[]{:S(2)}) %all-to-all-start.2) | async-done | bytes 131104 | tf_op jit(solution)/shard_map/all_to_all | solution.py:83
  77.1 1.3 convolution_bitcast_fusion.2
  78.3 1.2 convolution_bitcast_fusion.3
  79.6 1.5 fusion.33
  81.0 0.9 copy-done.10
  82.1 1.3 reduce.6
  83.4 0.7 reshape.172
  84.1 6.2 %all-to-all-start.3 = ((bf16[128,2,256]{2,1,0:T(2,128)(2,1)}), bf16[128,2,256]{2,1,0:T(2,128)(2,1)S(1)}, u32[]{:S(2)}, u32[]{:S(2)}) async-start(bf16[128,2,256]{2,1,0:T(2,128)(2,1)} %reshape.172), calls=%async_computation.3 | async-start | bytes 262144 | tf_op jit(solution)/shard_map/all_to_all | solution.py:82
  90.4 3.5 collective-permute-start.1
  93.9 2.3 collective-permute-start
  97.8 5.0 all-to-all-done.3
  103.1 170.6 %all-reduce.7.cloned.1.call-done = (f32[512,256]{0,1:T(8,128)}, f32[512,256]{0,1:T(8,128)}, f32[512,256]{0,1:T(8,128)}) async-done(((f32[512,256]{0,1:T(8,128)}, f32[512,256]{0,1:T(8,128)}, f32[512,256]{0,1:T(8,128)}), (f32[512,256]{0,1:T(8,128)}, f32[512,256]{0,1:T(8,128)}, f32[512,256]{0,1:T(8,128)})) %all-reduce.7.cloned.1.call-update) | async-done | bytes 1572880 | tf_op jit(solution)/shard_map/psum | solution.py:44
  273.7 1.4 multiply_reduce_fusion.3
  276.9 1.2 convolution_bitcast_fusion
  278.6 1.2 convolution_bitcast_fusion.1
  279.9 1.5 fusion.40
  283.0 196.7 %all-reduce.5.cloned.1.call-done = (f32[512,256]{0,1:T(8,128)}, f32[512,256]{0,1:T(8,128)}, f32[512,256]{0,1:T(8,128)}) async-done(((f32[512,256]{0,1:T(8,128)}, f32[512,256]{0,1:T(8,128)}, f32[512,256]{0,1:T(8,128)}), (f32[512,256]{0,1:T(8,128)}, f32[512,256]{0,1:T(8,128)}, f32[512,256]{0,1:T(8,128)})) %all-reduce.5.cloned.1.call-update) | async-done | bytes 1572880 | tf_op jit(solution)/shard_map/psum | solution.py:44
  479.7 1.2 multiply_reduce_fusion.1
  483.7 1.3 reduce.7
  485.7 11.5 %all-to-all-start.4 = ((bf16[128,2,256]{2,1,0:T(2,128)(2,1)}), bf16[128,2,256]{2,1,0:T(2,128)(2,1)S(1)}, u32[]{:S(2)}, u32[]{:S(2)}) async-start(bf16[128,2,256]{2,1,0:T(2,128)(2,1)} %reshape.174), calls=%async_computation.4 | async-start | bytes 262144 | tf_op jit(solution)/shard_map/all_to_all | solution.py:108
  497.6 11.9 %all-to-all-done.4 = bf16[128,2,256]{2,1,0:T(2,128)(2,1)S(1)} async-done(((bf16[128,2,256]{2,1,0:T(2,128)(2,1)}), bf16[128,2,256]{2,1,0:T(2,128)(2,1)S(1)}, u32[]{:S(2)}, u32[]{:S(2)}) %all-to-all-start.4) | async-done | bytes 131104 | tf_op jit(solution)/shard_map/all_to_all | solution.py:108
  509.6 0.9 fusion
  (84 shorter events, 15.3 us)
Async XLA Ops:
  6.5 19.9 %copy-start.11 = (bf16[128,512]{1,0:T(8,128)(2,1)S(1)}, bf16[128,512]{1,0:T(8,128)(2,1)}, u32[]{:S(2)}) copy-start(bf16[128,512]{1,0:T(8,128)(2,1)} %param.9) | copy-start | bytes 393220
  8.0 30.0 %all-to-all-start = ((bf16[1,128,1]{2,0,1:T(2,128)(2,1)}), bf16[1,128,1]{2,0,1:T(2,128)(2,1)S(1)}, u32[]{:S(2)}, u32[]{:S(2)}) async-start(bf16[1,128,1]{2,0,1:T(2,128)(2,1)} %copy.22), calls=%async_computation | async-start | bytes 131072 | tf_op jit(solution)/shard_map/all_to_all | solution.py:85
  29.1 14.6 %copy-start.9 = (bf16[128,512]{1,0:T(8,128)(2,1)S(1)}, bf16[128,512]{1,0:T(8,128)(2,1)}, u32[]{:S(2)}) copy-start(bf16[128,512]{1,0:T(8,128)(2,1)} %param.8) | copy-start | bytes 393220
  38.0 18.0 %all-to-all-start.1 = ((bf16[128,2,256]{2,1,0:T(2,128)(2,1)}), bf16[128,2,256]{2,1,0:T(2,128)(2,1)S(1)}, u32[]{:S(2)}, u32[]{:S(2)}) async-start(bf16[128,2,256]{2,1,0:T(2,128)(2,1)} %reshape.170), calls=%async_computation.1 | async-start | bytes 262144 | tf_op jit(solution)/shard_map/all_to_all | solution.py:84
  56.0 18.5 %all-to-all-start.2 = ((bf16[128,2,256]{2,1,0:T(2,128)(2,1)}), bf16[128,2,256]{2,1,0:T(2,128)(2,1)S(1)}, u32[]{:S(2)}, u32[]{:S(2)}) async-start(bf16[128,2,256]{2,1,0:T(2,128)(2,1)} %reshape.168), calls=%async_computation.2 | async-start | bytes 262144 | tf_op jit(solution)/shard_map/all_to_all | solution.py:83
  62.2 211.5 %all-reduce.7.cloned.1.call-start = ((), (), s32[]{:S(2)}) async-start(), calls=%async_computation.6 | async-start | bytes 3145728 | tf_op jit(solution)/shard_map/psum | solution.py:44
  74.6 1.0 copy-start.2
  74.9 1.0 copy-start.1
  75.9 0.9 copy-start
  81.0 0.9 copy-start.10
  84.1 18.6 %all-to-all-start.3 = ((bf16[128,2,256]{2,1,0:T(2,128)(2,1)}), bf16[128,2,256]{2,1,0:T(2,128)(2,1)S(1)}, u32[]{:S(2)}, u32[]{:S(2)}) async-start(bf16[128,2,256]{2,1,0:T(2,128)(2,1)} %reshape.172), calls=%async_computation.3 | async-start | bytes 262144 | tf_op jit(solution)/shard_map/all_to_all | solution.py:82
  90.3 389.4 %all-reduce.5.cloned.1.call-start = ((), (), s32[]{:S(2)}) async-start(), calls=%async_computation.5 | async-start | bytes 3145728 | tf_op jit(solution)/shard_map/psum | solution.py:44
  90.4 419.2 %collective-permute-start.1 = (bf16[128,512]{1,0:T(8,128)(2,1)S(1)}, bf16[128,512]{1,0:T(8,128)(2,1)S(1)}, u32[]{:S(2)}, u32[]{:S(2)}) collective-permute-start(bf16[128,512]{1,0:T(8,128)(2,1)S(1)} %copy-done.11), channel_id=1, source_target_pairs={{0,4},{4,8},{8,12},{12,16},{16,20},{20,24},{24,28},{28,32},{32,36}... | collective-permute-start | bytes 393224 | tf_op jit(solution)/shard_map/ppermute | solution.py:10
  93.9 403.3 %collective-permute-start = (bf16[128,512]{1,0:T(8,128)(2,1)S(1)}, bf16[128,512]{1,0:T(8,128)(2,1)S(1)}, u32[]{:S(2)}, u32[]{:S(2)}) collective-permute-start(bf16[128,512]{1,0:T(8,128)(2,1)S(1)} %copy-done.9), channel_id=1, source_target_pairs={{0,4},{4,8},{8,12},{12,16},{16,20},{20,24},{24,28},{28,32},{32,36}... | collective-permute-start | bytes 393224 | tf_op jit(solution)/shard_map/ppermute | solution.py:10
  273.7 1.4 copy-start.5
  275.2 1.0 copy-start.3
  276.9 1.3 copy-start.4
  479.7 1.2 copy-start.8
  479.7 1.4 copy-start.6
  481.1 1.0 copy-start.7
  485.7 11.6 %copy-start.12 = (pred[256]{0:T(512)(128)(4,1)S(1)}, pred[256]{0:T(512)(128)(4,1)}, u32[]{:S(2)}) copy-start(pred[256]{0:T(512)(128)(4,1)} %compare_or_fusion) | copy-start | bytes 772
  485.7 11.6 %copy-start.13 = (s32[128]{0:T(128)S(1)}, s32[128]{0:T(128)}, u32[]{:S(2)}) copy-start(s32[128]{0:T(128)} %iota_add_fusion) | copy-start | bytes 1540
  485.7 23.8 %all-to-all-start.4 = ((bf16[128,2,256]{2,1,0:T(2,128)(2,1)}), bf16[128,2,256]{2,1,0:T(2,128)(2,1)S(1)}, u32[]{:S(2)}, u32[]{:S(2)}) async-start(bf16[128,2,256]{2,1,0:T(2,128)(2,1)} %reshape.174), calls=%async_computation.4 | async-start | bytes 262144 | tf_op jit(solution)/shard_map/all_to_all | solution.py:108
Sparse Core Ops, SparseCore 0:
  81.2 192.5 all-reduce.6
  281.9 197.7 all-reduce.4
where the time goes:
time: 518 us; the launch traced here: 517 us
  waiting for transfers between devices  414 us (80%)
  starting transfers between devices  54.2 us (10%)
  matrix products  14.4 us (3%)
  between operations  13.8 us (3%)
  other arithmetic  11.2 us (2%)
  local copies, waits for them, and re-layouts  9.58 us (2%)
    psum x2, waiting for transfers between devices, descend(): g_gate, g_up, g_down = lax.psum((g_gate, g_up, g_down), 'seq')  367 us
    all_to_all x1, starting transfers between devices, local(): lax.all_to_all(spread(rates).astype(jnp.bfloat16), 'seq', split_axis=1, c...  18.4 us
    dot_general x18, matrix products, dot_high(): jnp.dot(a, b, precision=lax.Precision.HIGHEST, preferred_element_type=jnp...  13.3 us
    all_to_all x1, waiting for transfers between devices, local(): lax.all_to_all(sending, 'seq', split_axis=1, concat_axis=1, tiled=True)  11.9 us
    all_to_all x1, starting transfers between devices, local(): lax.all_to_all(sending, 'seq', split_axis=1, concat_axis=1, tiled=True)  11.5 us
    all_to_all x1, waiting for transfers between devices, local(): lax.all_to_all(spread(keys), 'seq', split_axis=1, concat_axis=1, tiled=True)  11.1 us
  transfers between devices with their start and end apart: 9, of which 7 were waited for; matrix products, arithmetic and copies ran while one was open for 5% of the time, Pallas kernels for 0%

commit v1 on v0

v1 whole, which is shorter than its diff:
```python
import functools
import math

import jax
import jax.numpy as jnp
from jax import lax
from jax.experimental import pallas as pl
from jax.experimental.pallas import tpu as pltpu
from jax.sharding import PartitionSpec as P

T = 128
DH = 512
FH = 256
HALF = 128
LANES = 128
NL = DH // LANES
ROWS = 3 * HALF
MESH = pl.DeviceIdType.MESH
F32 = jnp.float32
BF16 = jnp.bfloat16


def dot_nt(a, b):
    return lax.dot_general(a, b, (((1,), (1,)), ((), ())), preferred_element_type=F32)


def dot_nn(a, b):
    return jnp.dot(a, b, preferred_element_type=F32)


def split(a):
    high = a.astype(BF16)
    return high, (a - high.astype(F32)).astype(BF16)


def far_first(j, n):
    h = (j + 1) // 2
    return lax.rem(n // 2 + n + jnp.where(lax.rem(j, 2) == 1, -h, h), n)


def owner_row(k):
    return (k // 2) * 4 + 1 + lax.rem(k, 2)


def kernel(
    ny, nz,
    q_hbm, k_hbm, v_hbm, r_hbm, wg_hbm, wu_hbm, wd_hbm,
    out_ref,
    qq, kk, vv, hk, hv, r_in, rr, w_in, w_t, w_f, w_b,
    g_own, g_give, g_got, g_send0, g_send1, land0, land1, piece0, piece1, g_all0, g_all1,
    ss_own, ss_got, attn, f_give, f_got,
    in_sem, x_send, x_recv, h_send, h_recv, gh_send, gh_recv,
    rs_send, rs_recv, ag_send, ag_recv, ss_send, ss_recv, f_send, f_recv,
):
    s = lax.axis_index("seq")
    c = lax.rem(s, 2)
    chip = s // 2
    z = lax.rem(chip, nz)
    y = chip // nz
    half_y = ny // 2
    n_own = half_y * nz
    rows = ROWS * NL // n_own
    n_seq = ny * nz * 2
    span = y // half_y
    local_chip = chip - span * n_own
    is_owner0 = lax.rem((y + 1) // 2, 2) == 1
    own0 = (y + 3) // 4 * 2 - 2 + lax.rem(y + 3, 4)
    partner = s + 1 - 2 * c

    loads = [
        pltpu.make_async_copy(wg_hbm.at[0], w_in.at[0], in_sem.at[0]),
        pltpu.make_async_copy(wu_hbm.at[0], w_in.at[1], in_sem.at[1]),
        pltpu.make_async_copy(wd_hbm.at[0], w_in.at[2], in_sem.at[2]),
        pltpu.make_async_copy(k_hbm, kk.at[c], in_sem.at[3]),
        pltpu.make_async_copy(v_hbm, vv.at[c], in_sem.at[4]),
        pltpu.make_async_copy(r_hbm, r_in, in_sem.at[5]),
        pltpu.make_async_copy(q_hbm, qq.at[c], in_sem.at[6]),
    ]
    for load in loads:
        load.start()

    barrier = pltpu.get_barrier_semaphore()

    def greet(i, carry):
        zt = lax.rem(z + far_first(i // ny, nz), nz)
        yt = lax.rem(y + far_first(lax.rem(i, ny), ny), ny)
        target = (yt * nz + zt) * 2 + c

        @pl.when(target != s)
        def _():
            pl.semaphore_signal(barrier, inc=1, device_id={"seq": target}, device_id_type=MESH)

        return carry

    lax.fori_loop(0, ny * nz, greet, 0)
    pl.semaphore_signal(barrier, inc=1, device_id={"seq": partner}, device_id_type=MESH)
    beside = lax.rem(s + 2 * c - 1 + n_seq, n_seq)
    pl.semaphore_signal(barrier, inc=1, device_id={"seq": beside}, device_id_type=MESH)

    for m in range(3):
        loads[m].wait()
        w_t[m] = w_in[m].astype(F32).T.astype(BF16)
    for load in loads[3:]:
        load.wait()
    rr[c] = jnp.broadcast_to(r_in[...], (8, LANES))

    def activations(times, x, y_val, rate):
        h1 = times(0, x)
        h3 = times(1, x)
        dg = times(2, y_val) * (-rate)
        sig = jax.nn.sigmoid(h1)
        s1 = h1 * sig
        a_gate = dg * h3 * sig * (1.0 + h1 * (1.0 - sig))
        a_up = dg * s1
        a_down = (s1 * h3) * (-rate)
        return a_gate.astype(BF16), a_up.astype(BF16), a_down.astype(BF16)

    @pl.when(span == 0)
    def _():
        x, y_val = kk[c], vv[c]
        acts = activations(lambda m, a: dot_nt(w_t[m], a), x, y_val, rr[c][0:1])
        for m in range(3):
            grad = dot_nn(acts[m], x if m < 2 else y_val)
            low, high = grad[:HALF], grad[HALF:]
            mine = jnp.where(c == 0, low, high)
            theirs = jnp.where(c == 0, high, low).astype(BF16)
            for b in range(NL):
                g_own[b, m * HALF:(m + 1) * HALF, :] = mine[:, b * LANES:(b + 1) * LANES]
                g_give[b, m * HALF:(m + 1) * HALF, :] = theirs[:, b * LANES:(b + 1) * LANES]

    pl.semaphore_wait(barrier, ny * nz + 1)

    def to_partner(src, dst, send, recv):
        return pltpu.make_async_remote_copy(
            src_ref=src, dst_ref=dst, send_sem=send, recv_sem=recv, device_id={"seq": partner}, device_id_type=MESH
        )

    give = to_partner(g_give, g_got, gh_send, gh_recv)
    shares = [
        to_partner(ref.at[c], ref.at[c], x_send.at[i], x_recv.at[i]) for i, ref in enumerate((kk, vv, rr, qq))
    ]

    @pl.when(span == 0)
    def _():
        give.start()

    for share in shares:
        share.start()

    def block(ref, o):
        first = pl.multiple_of((o // NL) * rows, 16)
        return ref.at[lax.rem(o, NL), pl.ds(first, rows)]

    def scatter(src, land, y_of, phase):
        def send(i, carry):
            zt = lax.rem(z + far_first(i // half_y, nz), nz)
            k = lax.rem(i, half_y)
            target = (y_of(k) * nz + zt) * 2 + c
            from_ref, to_ref = block(src, k * nz + zt), land.at[local_chip]

            @pl.when(target == s)
            def _():
                pltpu.make_async_copy(from_ref, to_ref, rs_recv.at[phase]).start()

            @pl.when(target != s)
            def _():
                pltpu.make_async_remote_copy(
                    src_ref=from_ref, dst_ref=to_ref, send_sem=rs_send.at[phase], recv_sem=rs_recv.at[phase],
                    device_id={"seq": target}, device_id_type=MESH,
                ).start()

            return carry

        lax.fori_loop(0, n_own, send, 0)

    def reduce_piece(land, piece, phase):
        pltpu.make_async_copy(land, land, rs_recv.at[phase]).wait()
        total = land[0].astype(F32)
        for i in range(1, n_own):
            total = total + land[i].astype(F32)
        piece[...] = total.astype(BF16)

    def gather(piece, o, dst, first_y, sem, phase):
        def send(i, carry):
            zt = lax.rem(z + far_first(i // half_y, nz), nz)
            target = ((first_y + lax.rem(i, half_y)) * nz + zt) * 2 + c
            to_ref = block(dst, o)

            @pl.when(target == s)
            def _():
                pltpu.make_async_copy(piece, to_ref, ag_recv.at[phase]).start()

            @pl.when(target != s)
            def _():
                pltpu.make_async_remote_copy(
                    src_ref=piece, dst_ref=to_ref, send_sem=ag_send.at[sem], recv_sem=ag_recv.at[phase],
                    device_id={"seq": target}, device_id_type=MESH,
                ).start()

            return carry

        lax.fori_loop(0, n_own, send, 0)

    def wait_sent(sem, land, one_stayed):
        @pl.when(one_stayed)
        def _():
            part = land.at[pl.ds(0, n_own - 1)]
            pltpu.make_async_copy(part, part, sem).wait()

        @pl.when(jnp.logical_not(one_stayed))
        def _():
            pltpu.make_async_copy(land, land, sem).wait()

    @pl.when(span == 0)
    def _():
        give.wait_recv()
        g_send0[...] = (g_own[...] + g_got[...].astype(F32)).astype(BF16)
        scatter(g_send0, land0, owner_row, 0)

    halo = [
        pltpu.make_async_remote_copy(
            src_ref=src.at[c], dst_ref=dst, send_sem=h_send.at[i], recv_sem=h_recv.at[i],
            device_id={"seq": beside}, device_id_type=MESH,
        )
        for i, (src, dst) in enumerate(((kk, hk), (vv, hv)))
    ]

    def attention():
        @pl.when(c == 1)
        def _():
            for copy in halo:
                copy.start()

        for share in shares:
            share.wait_recv()

        @pl.when(c == 0)
        def _():
            for copy in halo:
                copy.wait_recv()

        @pl.when(c == 1)
        def _():
            hk[...] = kk[0]
            hv[...] = vv[0]

        q = qq[c]
        inv = jnp.sqrt(jnp.float32(DH))
        before = dot_nt(q, hk[...]) / inv
        here = dot_nt(q, kk[c]) / inv
        row = lax.broadcasted_iota(jnp.int32, (T, T), 0)
        col = lax.broadcasted_iota(jnp.int32, (T, T), 1)
        before = jnp.where((col > row) & (s > 0), before, jnp.float32(-1e30))
        here = jnp.where(col <= row, here, jnp.float32(-1e30))
        top = jnp.maximum(jnp.max(before, axis=1, keepdims=True), jnp.max(here, axis=1, keepdims=True))
        before, here = jnp.exp(before - top), jnp.exp(here - top)
        norm = jnp.sum(before, axis=1, keepdims=True) + jnp.sum(here, axis=1, keepdims=True)
        before, here = (before / norm).astype(BF16), (here / norm).astype(BF16)
        attn[...] = dot_nn(before, hv[...]) + dot_nn(here, vv[c])

    @pl.when(span == 1)
    def _():
        attention()

    @pl.when(is_owner0)
    def _():
        reduce_piece(land0, piece0, 0)
        o = own0 * nz + z
        gather(piece0, o, g_all0, half_y, 0, 0)
        gather(piece0, o, g_all0, 0, 1, 0)

    @pl.when(span == 0)
    def _():
        attention()

    def descend(phase, g_all, old):
        pltpu.make_async_copy(g_all, g_all, ag_recv.at[phase]).wait()
        ss_own[phase] = jnp.zeros((16, LANES), F32)
        for m in range(3):
            for b in range(NL):
                g = g_all[b, m * HALF:(m + 1) * HALF, :].astype(F32)
                ss_own[phase, m * NL + b:m * NL + b + 1, :] = jnp.sum(g * g, axis=0, keepdims=True)
        swap = to_partner(ss_own.at[phase], ss_got.at[phase], ss_send.at[phase], ss_recv.at[phase])
        swap.start()
        swap.wait()
        scale = 0.05 * lax.rsqrt((ss_own[phase] + ss_got[phase]) * (1.0 / FH) + 1e-06)
        for m in range(3):
            for b in range(NL):
                g = g_all[b, m * HALF:(m + 1) * HALF, :].astype(F32)
                j = m * NL + b
                new = old(m, b) - g * scale[j:j + 1]
                w_f[b, m * HALF:(m + 1) * HALF, :] = new
                for i, term in enumerate(split(new)):
                    w_b[i, m * HALF:(m + 1) * HALF, b * LANES:(b + 1) * LANES] = term

    first = pl.multiple_of(c * HALF, HALF)
    descend(0, g_all0, lambda m, b: w_t[m, pl.ds(first, HALF), b * LANES:(b + 1) * LANES].astype(F32))

    @pl.when(span == 1)
    def _():
        x, y_val = kk[...].reshape(2 * T, DH), vv[...].reshape(2 * T, DH)
        rate = jnp.concatenate([rr[0][0:1], rr[1][0:1]], axis=1)
        acts = activations(
            lambda m, a: dot_nt(w_b[0, m * HALF:(m + 1) * HALF], a) + dot_nt(w_b[1, m * HALF:(m + 1) * HALF], a),
            x, y_val, rate,
        )
        for m in range(3):
            grad = dot_nn(acts[m], x if m < 2 else y_val).astype(BF16)
            for b in range(NL):
                g_send1[b, m * HALF:(m + 1) * HALF, :] = grad[:, b * LANES:(b + 1) * LANES]
        scatter(g_send1, land1, lambda k: half_y + k, 1)
        reduce_piece(land1, piece1, 1)
        gather(piece1, local_chip, g_all1, half_y, 2, 1)
        descend(1, g_all1, lambda m, b: w_f[b, m * HALF:(m + 1) * HALF, :])

    q_all = qq[...].reshape(2 * T, DH)
    h1 = dot_nt(q_all, w_b[0, 0:HALF]) + dot_nt(q_all, w_b[1, 0:HALF])
    h3 = dot_nt(q_all, w_b[0, HALF:2 * HALF]) + dot_nt(q_all, w_b[1, HALF:2 * HALF])
    high, low = split(h1 * jax.nn.sigmoid(h1) * h3)
    w_high, w_low = w_b[0, 2 * HALF:ROWS], w_b[1, 2 * HALF:ROWS]
    f = dot_nn(high, w_high) + (dot_nn(low, w_high) + dot_nn(high, w_low))
    mine = jnp.where(c == 0, f[:T], f[T:])
    f_give[...] = jnp.where(c == 0, f[T:], f[:T])
    swap = to_partner(f_give, f_got, f_send, f_recv)
    swap.start()
    swap.wait()
    f = mine + f_got[...]
    fast = (f * lax.rsqrt(jnp.mean(f * f, axis=1, keepdims=True) + 1e-06)).astype(BF16)
    out_ref[...] = (attn[...] + fast.astype(F32)).astype(BF16)

    for share in shares:
        share.wait_send()

    @pl.when(c == 1)
    def _():
        for copy in halo:
            copy.wait_send()

    @pl.when(span == 0)
    def _():
        give.wait_send()
        wait_sent(rs_send.at[0], land0, is_owner0)

    @pl.when(is_owner0)
    def _():
        wait_sent(ag_send.at[0], land0, span == 1)
        wait_sent(ag_send.at[1], land0, span == 0)

    @pl.when(span == 1)
    def _():
        wait_sent(rs_send.at[1], land1, span == 1)
        wait_sent(ag_send.at[2], land1, span == 1)


def local(ny, nz, queries, keys, values, rates, gate_fast, up_fast, down_fast):
    n_own = ny // 2 * nz
    rows = ROWS * NL // n_own
    dma = pltpu.SemaphoreType.DMA
    full = (NL, ROWS, LANES)
    return pl.pallas_call(
        functools.partial(kernel, ny, nz),
        out_shape=jax.ShapeDtypeStruct((T, DH), BF16),
        in_specs=[pl.BlockSpec(memory_space=pl.ANY)] * 7,
        out_specs=pl.BlockSpec(memory_space=pltpu.VMEM),
        scratch_shapes=[
            pltpu.VMEM((2, T, DH), BF16),
            pltpu.VMEM((2, T, DH), BF16),
            pltpu.VMEM((2, T, DH), BF16),
            pltpu.VMEM((T, DH), BF16),
            pltpu.VMEM((T, DH), BF16),
            pltpu.VMEM((1, T), F32),
            pltpu.VMEM((2, 8, LANES), F32),
            pltpu.VMEM((3, DH, FH), BF16),
            pltpu.VMEM((3, FH, DH), BF16),
            pltpu.VMEM(full, F32),
            pltpu.VMEM((2, ROWS, DH), BF16),
            pltpu.VMEM(full, F32),
            pltpu.VMEM(full, BF16),
            pltpu.VMEM(full, BF16),
            pltpu.VMEM(full, BF16),
            pltpu.VMEM(full, BF16),
            pltpu.VMEM((n_own, rows, LANES), BF16),
            pltpu.VMEM((n_own, rows, LANES), BF16),
            pltpu.VMEM((rows, LANES), BF16),
            pltpu.VMEM((rows, LANES), BF16),
            pltpu.VMEM(full, BF16),
            pltpu.VMEM(full, BF16),
            pltpu.VMEM((2, 16, LANES), F32),
            pltpu.VMEM((2, 16, LANES), F32),
            pltpu.VMEM((T, DH), F32),
            pltpu.VMEM((T, DH), F32),
            pltpu.VMEM((T, DH), F32),
            dma((7,)),
            dma((4,)),
            dma((4,)),
            dma((2,)),
            dma((2,)),
            dma,
            dma,
            dma((2,)),
            dma((2,)),
            dma((3,)),
            dma((2,)),
            dma((2,)),
            dma((2,)),
            dma,
            dma,
        ],
        compiler_params=pltpu.CompilerParams(
            collective_id=0, has_side_effects=True, vmem_limit_bytes=60 * 2**20
        ),
        name="fast_layer",
    )(queries, keys, values, rates.reshape(1, T), gate_fast, up_fast, down_fast)


def solution(mesh):
    n_chips = mesh.shape["seq"] // 2
    ny = 1 << ((n_chips.bit_length()) // 2)
    nz = n_chips // ny
    return jax.shard_map(
        functools.partial(local, ny, nz),
        mesh=mesh,
        in_specs=(
            P("seq", "head"),
            P("seq", "head"),
            P("seq", "head"),
            P("seq", "head"),
            P("head", None, None),
            P("head", None, None),
            P("head", None, None),
        ),
        out_specs=P("seq", "head"),
        check_vma=False,
    )
```

time: 518 us -> 80.1 us (0.15)
  the two profiles are of different devices: /device:TPU:1 before, /device:TPU:49 now
where the time goes in v1:
time: 80.1 us; the launch traced here: 80 us
  Pallas kernels  78.4 us (98%)
  local copies, waits for them, and re-layouts  1.57 us (2%)
    pallas_call x1, Pallas kernels, local(): pl.pallas_call(functools.partial(kernel, ny, nz), out_shape=jax.ShapeDtyp...  78.4 us

profile of v1, /device:TPU:49, one launch (start us, length us, event | category | flops | bytes accessed | tf_op | source)
XLA Modules:
  0.0 80.0 jit_solution(5710693285777523280)
XLA Ops:
  0.0 78.4 %fast_layer.1 = bf16[128,512]{1,0:T(8,128)(2,1)} custom-call(bf16[128,512]{1,0:T(8,128)(2,1)} %q_hbm.1, bf16[128,512]{1,0:T(8,128)(2,1)} %k_hbm.1, bf16[128,512]{1,0:T(8,128)(2,1)} %v_hbm.1, f32[1,128]{1,0:T(1,128)} %bitcast.1, bf16[1,512,256]{2,1,0:T(8,128)(2,1)} %wg_hbm.1, bf16[1,512,256]{2,1,0:T(8,128)(2,1)} %wu_hbm.1, bf16[1,512,256]{2,1,0:T(8,128)(2,1)} %wd_hbm.1), custom_call_target="tpu_custom_call" | custom-call | tf_op jit(solution)/shard_map/fast_layer/pallas_call | solution.py:360
  78.4 1.6 %copy.9 = bf16[128,512]{1,0:T(8,128)(2,1)} copy(bf16[128,512]{1,0:T(8,128)(2,1)} %fast_layer.1) | data formatting | bytes 262144

commit v2 on v1

v2 whole, which is shorter than its diff:
```python
import functools
import math

import jax
import jax.numpy as jnp
from jax import lax
from jax.experimental import pallas as pl
from jax.experimental.pallas import tpu as pltpu
from jax.sharding import PartitionSpec as P

T = 128
DH = 512
FH = 256
HALF = 128
LANES = 128
NL = DH // LANES
ROWS = 3 * HALF
MESH = pl.DeviceIdType.MESH
F32 = jnp.float32
BF16 = jnp.bfloat16


def dot_nt(a, b):
    return lax.dot_general(a, b, (((1,), (1,)), ((), ())), preferred_element_type=F32)


def dot_nn(a, b):
    return jnp.dot(a, b, preferred_element_type=F32)


def split(a):
    high = a.astype(BF16)
    return high, (a - high.astype(F32)).astype(BF16)


def far_first(j, n):
    h = (j + 1) // 2
    return lax.rem(n // 2 + n + jnp.where(lax.rem(j, 2) == 1, -h, h), n)


def far_offsets(n):
    return sorted(range(1, n), key=lambda d: -min(d, n - d))


def kernel(
    ny, nz,
    q_hbm, k_hbm, v_hbm, r_hbm, wg_hbm, wu_hbm, wd_hbm,
    out_ref,
    qq, kk, vv, hk, hv, r_in, rr, w_in, w_f, w_b,
    g_own, g_give, g_got, g_send0, g_send1, g_all0, g_all1,
    landz0, landz1, midz0, midz1, finy0, finy1, landy0, landy1, midy0, midy1, finz0, finz1, piece0, piece1,
    ss_own, ss_got, attn, f_give, f_got,
    in_sem, x_send, x_recv, h_send, h_recv, gh_send, gh_recv,
    rs_send, rs_recv, ag_send, ag_recv, ss_send, ss_recv, f_send, f_recv,
):
    s = lax.axis_index("seq")
    c = lax.rem(s, 2)
    chip = s // 2
    z = lax.rem(chip, nz)
    y = chip // nz
    half_y = ny // 2
    rows = ROWS // nz
    nb = NL // half_y
    n_seq = ny * nz * 2
    span = y // half_y
    local_y = y - span * half_y
    partner = s + 1 - 2 * c
    owner0 = jnp.where(c == 0, span == 0, lax.rem((y + 1) // 2, 2) == 1)
    own0 = jnp.where(c == 0, local_y, (y + 3) // 4 * 2 - 2 + lax.rem(y + 3, 4))

    def row0(k):
        return jnp.where(c == 0, k, (k // 2) * 4 + 1 + lax.rem(k, 2))

    def row1(k):
        return half_y + k

    def seq_at(row, column):
        return (row * nz + column) * 2 + c

    loads = [
        pltpu.make_async_copy(k_hbm, kk.at[c], in_sem.at[0]),
        pltpu.make_async_copy(v_hbm, vv.at[c], in_sem.at[1]),
        pltpu.make_async_copy(r_hbm, r_in, in_sem.at[2]),
        pltpu.make_async_copy(wg_hbm.at[0], w_in.at[0], in_sem.at[3]),
        pltpu.make_async_copy(wu_hbm.at[0], w_in.at[1], in_sem.at[4]),
        pltpu.make_async_copy(wd_hbm.at[0], w_in.at[2], in_sem.at[5]),
        pltpu.make_async_copy(q_hbm, qq.at[c], in_sem.at[6]),
    ]
    for load in loads:
        load.start()

    barrier = pltpu.get_barrier_semaphore()

    def greet(target):
        pl.semaphore_signal(barrier, inc=1, device_id={"seq": target}, device_id_type=MESH)

    for i in range(ny - 1):
        greet(seq_at(lax.rem(y + far_offsets(ny)[i], ny), z))
    for i in range(nz - 1):
        greet(seq_at(y, lax.rem(z + far_offsets(nz)[i], nz)))
    beside = lax.rem(s + 2 * c - 1 + n_seq, n_seq)
    greet(beside)
    greet(partner)

    for load in loads:
        load.wait()
    rr[c] = jnp.broadcast_to(r_in[...], (8, LANES))

    def slopes(h1, h3, dg, rate):
        sig = jax.nn.sigmoid(h1)
        s1 = h1 * sig
        a_gate = dg * h3 * sig * (1.0 + h1 * (1.0 - sig))
        return a_gate, dg * s1, (s1 * h3) * rate

    @pl.when(span == 0)
    def _():
        x, y_val = kk[c], vv[c]
        minus_r = -jnp.broadcast_to(r_in[...], (LANES, T)).T[:, 0:1]
        acts = slopes(dot_nn(x, w_in[0]), dot_nn(x, w_in[1]), dot_nn(y_val, w_in[2]) * minus_r, minus_r)
        for m in range(3):
            grad = dot_nn(acts[m].T.astype(BF16), x if m < 2 else y_val)
            low, high = grad[:HALF], grad[HALF:]
            mine = jnp.where(c == 0, low, high)
            theirs = jnp.where(c == 0, high, low).astype(BF16)
            for b in range(NL):
                g_own[b, m * HALF:(m + 1) * HALF, :] = mine[:, b * LANES:(b + 1) * LANES]
                g_give[b, m * HALF:(m + 1) * HALF, :] = theirs[:, b * LANES:(b + 1) * LANES]

    pl.semaphore_wait(barrier, ny + nz)

    def remote(src, dst, send, recv, target):
        return pltpu.make_async_remote_copy(
            src_ref=src, dst_ref=dst, send_sem=send, recv_sem=recv, device_id={"seq": target}, device_id_type=MESH
        )

    give = remote(g_give, g_got, gh_send, gh_recv, partner)
    shares = [
        remote(ref.at[c], ref.at[c], x_send.at[i], x_recv.at[i], partner) for i, ref in enumerate((kk, vv, rr, qq))
    ]

    @pl.when(span == 0)
    def _():
        give.start()

    for share in shares:
        share.start()

    def fan(n, place, src, dst, send, recv):
        def one(i, carry):
            index, target = place(i)
            from_ref, to_ref = src(index), dst(index)

            @pl.when(target == s)
            def _():
                pltpu.make_async_copy(from_ref, to_ref, recv).start()

            @pl.when(target != s)
            def _():
                remote(from_ref, to_ref, send, recv, target).start()

            return carry

        lax.fori_loop(0, n, one, 0)

    def along_z(i):
        zt = lax.rem(z + far_first(i, nz), nz)
        return zt, seq_at(y, zt)

    def along_y(row_of):
        def place(i):
            k = lax.rem(i + y + 1, half_y)
            return k, seq_at(row_of(k), z)

        return place

    def part(column):
        return pl.ds(pl.multiple_of(column * rows, 16), rows)

    def lanes(k):
        return pl.ds(k * nb, nb)

    def arrived(ref, sem):
        pltpu.make_async_copy(ref, ref, sem).wait()

    def total(ref):
        out = ref[0].astype(F32)
        for i in range(1, ref.shape[0]):
            out = out + ref[i].astype(F32)
        return out.astype(BF16)

    def scatter_first(p, g_send, landz, landy, row_of):
        @pl.when(c == 0)
        def _():
            fan(nz, along_z, lambda zt: g_send.at[:, part(zt)], lambda zt: landz.at[z], rs_send.at[p, 0], rs_recv.at[p, 0])

        @pl.when(c == 1)
        def _():
            fan(half_y, along_y(row_of), lambda k: g_send.at[lanes(k)], lambda k: landy.at[local_y],
                rs_send.at[p, 0], rs_recv.at[p, 0])

    def scatter_second(p, in_span, owner, landz, midz, finy, landy, midy, finz, piece, row_of):
        @pl.when((c == 0) & in_span)
        def _():
            arrived(landz, rs_recv.at[p, 0])
            midz[...] = total(landz)
            fan(half_y, along_y(row_of), lambda k: midz.at[lanes(k)], lambda k: finy.at[local_y],
                rs_send.at[p, 1], rs_recv.at[p, 1])

        @pl.when((c == 0) & owner)
        def _():
            arrived(finy, rs_recv.at[p, 1])
            piece[...] = total(finy)

        @pl.when((c == 1) & owner)
        def _():
            arrived(landy, rs_recv.at[p, 0])
            midy[...] = total(landy)
            fan(nz, along_z, lambda zt: midy.at[:, part(zt)], lambda zt: finz.at[z], rs_send.at[p, 1], rs_recv.at[p, 1])
            arrived(finz, rs_recv.at[p, 1])
            piece[...] = total(finz)

    def gather(p, owner, own, piece, g_all, first_rows):
        @pl.when((c == 0) & owner)
        def _():
            for i, first in enumerate(first_rows):
                fan(half_y, along_y(lambda k: first + k), lambda k: piece, lambda k: g_all.at[lanes(own), part(z)],
                    ag_send.at[p, i], ag_recv.at[p, 0])

        @pl.when(c == 0)
        def _():
            arrived(g_all.at[:, part(z)], ag_recv.at[p, 0])

            def one(i, carry):
                zt, target = along_z(i)
                remote(g_all.at[:, part(z)], g_all.at[:, part(z)], ag_send.at[p, 2], ag_recv.at[p, 1], target).start()
                return carry

            lax.fori_loop(0, nz - 1, one, 0)

        @pl.when((c == 1) & owner)
        def _():
            fan(nz, along_z, lambda zt: piece, lambda zt: g_all.at[lanes(own), part(z)], ag_send.at[p, 0], ag_recv.at[p, 0])
            arrived(g_all.at[lanes(own)], ag_recv.at[p, 0])
            for i, first in enumerate(first_rows):

                def one(j, carry):
                    k, target = along_y(lambda k: first + k)(j)

                    @pl.when(target != s)
                    def _():
                        remote(g_all.at[lanes(own)], g_all.at[lanes(own)], ag_send.at[p, 1 + i], ag_recv.at[p, 1], target).start()

                    return carry

                lax.fori_loop(0, half_y, one, 0)

    def gathered(p, owner, g_all):
        @pl.when(c == 0)
        def _():
            arrived(g_all.at[:, pl.ds(0, ROWS - rows)], ag_recv.at[p, 1])

        @pl.when((c == 1) & owner)
        def _():
            arrived(g_all.at[pl.ds(0, NL - nb)], ag_recv.at[p, 1])

        @pl.when((c == 1) & jnp.logical_not(owner))
        def _():
            arrived(g_all, ag_recv.at[p, 1])

    first = pl.multiple_of(c * HALF, HALF)

    def initial_weights():
        for m in range(3):
            w = w_in[m, :, pl.ds(first, HALF)].astype(F32).T
            for b in range(NL):
                w_f[b, m * HALF:(m + 1) * HALF, :] = w[:, b * LANES:(b + 1) * LANES]

    halo = [
        remote(src.at[c], dst, h_send.at[i], h_recv.at[i], beside) for i, (src, dst) in enumerate(((kk, hk), (vv, hv)))
    ]

    def attention():
        @pl.when(c == 1)
        def _():
            for copy in halo:
                copy.start()

        for share in shares:
            share.wait_recv()

        @pl.when(c == 0)
        def _():
            for copy in halo:
                copy.wait_recv()

        @pl.when(c == 1)
        def _():
            hk[...] = kk[0]
            hv[...] = vv[0]

        q = qq[c]
        inv = jnp.sqrt(jnp.float32(DH))
        before = dot_nt(q, hk[...]) / inv
        here = dot_nt(q, kk[c]) / inv
        row = lax.broadcasted_iota(jnp.int32, (T, T), 0)
        col = lax.broadcasted_iota(jnp.int32, (T, T), 1)
        before = jnp.where((col > row) & (s > 0), before, jnp.float32(-1e30))
        here = jnp.where(col <= row, here, jnp.float32(-1e30))
        top = jnp.maximum(jnp.max(before, axis=1, keepdims=True), jnp.max(here, axis=1, keepdims=True))
        before, here = jnp.exp(before - top), jnp.exp(here - top)
        norm = jnp.sum(before, axis=1, keepdims=True) + jnp.sum(here, axis=1, keepdims=True)
        before, here = (before / norm).astype(BF16), (here / norm).astype(BF16)
        attn[...] = dot_nn(before, hv[...]) + dot_nn(here, vv[c])

    @pl.when(span == 0)
    def _():
        give.wait_recv()
        g_send0[...] = (g_own[...] + g_got[...].astype(F32)).astype(BF16)
        scatter_first(0, g_send0, landz0, landy0, row0)

    initial_weights()

    @pl.when(span == 1)
    def _():
        attention()

    scatter_second(0, span == 0, owner0, landz0, midz0, finy0, landy0, midy0, finz0, piece0, row0)
    gather(0, owner0, own0, piece0, g_all0, (half_y, 0))

    @pl.when(span == 0)
    def _():
        attention()

    def descend(p, g_all):
        ss_own[p] = jnp.zeros((16, LANES), F32)
        for m in range(3):
            for b in range(NL):
                g = g_all[b, m * HALF:(m + 1) * HALF, :].astype(F32)
                ss_own[p, m * NL + b:m * NL + b + 1, :] = jnp.sum(g * g, axis=0, keepdims=True)
        swap = remote(ss_own.at[p], ss_got.at[p], ss_send.at[p], ss_recv.at[p], partner)
        swap.start()
        swap.wait()
        scale = 0.05 * lax.rsqrt((ss_own[p] + ss_got[p]) * (1.0 / FH) + 1e-06)
        for m in range(3):
            for b in range(NL):
                g = g_all[b, m * HALF:(m + 1) * HALF, :].astype(F32)
                j = m * NL + b
                new = w_f[b, m * HALF:(m + 1) * HALF, :] - g * scale[j:j + 1]
                w_f[b, m * HALF:(m + 1) * HALF, :] = new
                for i, term in enumerate(split(new)):
                    w_b[i, m * HALF:(m + 1) * HALF, b * LANES:(b + 1) * LANES] = term

    gathered(0, owner0, g_all0)
    descend(0, g_all0)

    @pl.when(span == 1)
    def _():
        x, y_val = kk[...].reshape(2 * T, DH), vv[...].reshape(2 * T, DH)
        minus_r = -jnp.concatenate([rr[0][0:1], rr[1][0:1]], axis=1)

        def times(m, a):
            return dot_nt(w_b[0, m * HALF:(m + 1) * HALF], a) + dot_nt(w_b[1, m * HALF:(m + 1) * HALF], a)

        acts = slopes(times(0, x), times(1, x), times(2, y_val) * minus_r, minus_r)
        for m in range(3):
            grad = dot_nn(acts[m].astype(BF16), x if m < 2 else y_val).astype(BF16)
            for b in range(NL):
                g_send1[b, m * HALF:(m + 1) * HALF, :] = grad[:, b * LANES:(b + 1) * LANES]
        scatter_first(1, g_send1, landz1, landy1, row1)
        scatter_second(1, True, True, landz1, midz1, finy1, landy1, midy1, finz1, piece1, row1)
        gather(1, True, local_y, piece1, g_all1, (half_y,))
        gathered(1, True, g_all1)
        descend(1, g_all1)

    def apply():
        q_all = qq[...].reshape(2 * T, DH)
        h1 = dot_nt(q_all, w_b[0, 0:HALF]) + dot_nt(q_all, w_b[1, 0:HALF])
        h3 = dot_nt(q_all, w_b[0, HALF:2 * HALF]) + dot_nt(q_all, w_b[1, HALF:2 * HALF])
        high, low = split(h1 * jax.nn.sigmoid(h1) * h3)
        w_high, w_low = w_b[0, 2 * HALF:ROWS], w_b[1, 2 * HALF:ROWS]
        f = dot_nn(high, w_high) + (dot_nn(low, w_high) + dot_nn(high, w_low))
        mine = jnp.where(c == 0, f[:T], f[T:])
        f_give[...] = jnp.where(c == 0, f[T:], f[:T])
        swap = remote(f_give, f_got, f_send, f_recv, partner)
        swap.start()
        swap.wait()
        f = mine + f_got[...]
        fast = (f * lax.rsqrt(jnp.mean(f * f, axis=1, keepdims=True) + 1e-06)).astype(BF16)
        out_ref[...] = (attn[...] + fast.astype(F32)).astype(BF16)

    apply()

    for share in shares:
        share.wait_send()

    @pl.when(c == 1)
    def _():
        for copy in halo:
            copy.wait_send()

    def left(sem, land, one_stayed):
        if one_stayed is True:
            arrived(land.at[pl.ds(0, land.shape[0] - 1)], sem)
            return

        @pl.when(one_stayed)
        def _():
            arrived(land.at[pl.ds(0, land.shape[0] - 1)], sem)

        @pl.when(jnp.logical_not(one_stayed))
        def _():
            arrived(land, sem)

    def all_left(p, in_span, owner, landz, finy, landy, finz, spans):
        @pl.when((c == 0) & in_span)
        def _():
            left(rs_send.at[p, 0], landz, True)
            left(rs_send.at[p, 1], finy, owner)

        @pl.when((c == 1) & in_span)
        def _():
            left(rs_send.at[p, 0], landy, owner)

        @pl.when((c == 0) & owner)
        def _():
            for i, k in enumerate(spans):
                left(ag_send.at[p, i], finy, span == k)

        @pl.when(c == 0)
        def _():
            left(ag_send.at[p, 2], landz, True)

        @pl.when((c == 1) & owner)
        def _():
            left(rs_send.at[p, 1], finz, True)
            left(ag_send.at[p, 0], finz, True)
            for i, k in enumerate(spans):
                left(ag_send.at[p, 1 + i], landy, span == k)

    @pl.when(span == 0)
    def _():
        give.wait_send()

    all_left(0, span == 0, owner0, landz0, finy0, landy0, finz0, (1, 0))

    @pl.when(span == 1)
    def _():
        all_left(1, True, True, landz1, finy1, landy1, finz1, (1,))


def local(ny, nz, queries, keys, values, rates, gate_fast, up_fast, down_fast):
    rows = ROWS // nz
    half_y = ny // 2
    nb = NL // half_y
    dma = pltpu.SemaphoreType.DMA
    full = (NL, ROWS, LANES)

    def twice(*shape):
        return [pltpu.VMEM(shape, BF16)] * 2

    return pl.pallas_call(
        functools.partial(kernel, ny, nz),
        out_shape=jax.ShapeDtypeStruct((T, DH), BF16),
        in_specs=[pl.BlockSpec(memory_space=pl.ANY)] * 7,
        out_specs=pl.BlockSpec(memory_space=pltpu.VMEM),
        scratch_shapes=[
            pltpu.VMEM((2, T, DH), BF16),
            pltpu.VMEM((2, T, DH), BF16),
            pltpu.VMEM((2, T, DH), BF16),
            pltpu.VMEM((T, DH), BF16),
            pltpu.VMEM((T, DH), BF16),
            pltpu.VMEM((1, T), F32),
            pltpu.VMEM((2, 8, LANES), F32),
            pltpu.VMEM((3, DH, FH), BF16),
            pltpu.VMEM(full, F32),
            pltpu.VMEM((2, ROWS, DH), BF16),
            pltpu.VMEM(full, F32),
            pltpu.VMEM(full, BF16),
            pltpu.VMEM(full, BF16),
            *twice(*full),
            *twice(*full),
            *twice(nz, NL, rows, LANES),
            *twice(NL, rows, LANES),
            *twice(half_y, nb, rows, LANES),
            *twice(half_y, nb, ROWS, LANES),
            *twice(nb, ROWS, LANES),
            *twice(nz, nb, rows, LANES),
            *twice(nb, rows, LANES),
            pltpu.VMEM((2, 16, LANES), F32),
            pltpu.VMEM((2, 16, LANES), F32),
            pltpu.VMEM((T, DH), F32),
            pltpu.VMEM((T, DH), F32),
            pltpu.VMEM((T, DH), F32),
            dma((7,)),
            dma((4,)),
            dma((4,)),
            dma((2,)),
            dma((2,)),
            dma,
            dma,
            dma((2, 2)),
            dma((2, 2)),
            dma((2, 3)),
            dma((2, 2)),
            dma((2,)),
            dma((2,)),
            dma,
            dma,
        ],
        compiler_params=pltpu.CompilerParams(
            collective_id=0, has_side_effects=True, vmem_limit_bytes=60 * 2**20
        ),
        name="fast_layer",
    )(queries, keys, values, rates.reshape(1, T), gate_fast, up_fast, down_fast)


def solution(mesh):
    n_chips = mesh.shape["seq"] // 2
    ny = 1 << ((n_chips.bit_length()) // 2)
    nz = n_chips // ny
    return jax.shard_map(
        functools.partial(local, ny, nz),
        mesh=mesh,
        in_specs=(
            P("seq", "head"),
            P("seq", "head"),
            P("seq", "head"),
            P("seq", "head"),
            P("head", None, None),
            P("head", None, None),
            P("head", None, None),
        ),
        out_specs=P("seq", "head"),
        check_vma=False,
    )
```

time: 80.1 us -> 70 us (0.87)
  the two profiles are of different devices: /device:TPU:49 before, /device:TPU:61 now
where the time goes in v2:
time: 70 us; the launch traced here: 69.9 us
  Pallas kernels  68.3 us (98%)
  local copies, waits for them, and re-layouts  1.57 us (2%)
    pallas_call x1, Pallas kernels, local(): pl.pallas_call(functools.partial(kernel, ny, nz), out_shape=jax.ShapeDtyp...  68.3 us
    unnamed x1, local copies, waits for them, and re-layouts  1.57 us

profile of v2, /device:TPU:61, one launch (start us, length us, event | category | flops | bytes accessed | tf_op | source)
XLA Modules:
  0.0 69.9 jit_solution(15648849393047983927)
XLA Ops:
  0.0 68.3 %fast_layer.1 = bf16[128,512]{1,0:T(8,128)(2,1)} custom-call(bf16[128,512]{1,0:T(8,128)(2,1)} %q_hbm.1, bf16[128,512]{1,0:T(8,128)(2,1)} %k_hbm.1, bf16[128,512]{1,0:T(8,128)(2,1)} %v_hbm.1, f32[1,128]{1,0:T(1,128)} %bitcast.1, bf16[1,512,256]{2,1,0:T(8,128)(2,1)} %wg_hbm.1, bf16[1,512,256]{2,1,0:T(8,128)(2,1)} %wu_hbm.1, bf16[1,512,256]{2,1,0:T(8,128)(2,1)} %wd_hbm.1), custom_call_target="tpu_custom_call" | custom-call | tf_op jit(solution)/shard_map/fast_layer/pallas_call | solution.py:461
  68.3 1.6 %copy.9 = bf16[128,512]{1,0:T(8,128)(2,1)} copy(bf16[128,512]{1,0:T(8,128)(2,1)} %fast_layer.1) | data formatting | bytes 262144

commit v3 on v2

v3 whole, which is shorter than its diff:
```python
import functools
import math

import jax
import jax.numpy as jnp
from jax import lax
from jax.experimental import pallas as pl
from jax.experimental.pallas import tpu as pltpu
from jax.sharding import PartitionSpec as P

T = 128
DH = 512
FH = 256
HALF = 128
LANES = 128
NL = DH // LANES
NK = 4
BLOCK = HALF // NK
ROWS = NL * 3 * BLOCK
MESH = pl.DeviceIdType.MESH
F32 = jnp.float32
BF16 = jnp.bfloat16


def dot_nt(a, b):
    return lax.dot_general(a, b, (((1,), (1,)), ((), ())), preferred_element_type=F32)


def dot_nn(a, b):
    return jnp.dot(a, b, preferred_element_type=F32)


def split(a):
    high = a.astype(BF16)
    return high, (a - high.astype(F32)).astype(BF16)


def far_first(j, n):
    h = (j + 1) // 2
    return lax.rem(n // 2 + n + jnp.where(lax.rem(j, 2) == 1, -h, h), n)


def far_offsets(n):
    return sorted(range(1, n), key=lambda d: -min(d, n - d))


def kernel(
    ny, nz,
    q_hbm, k_hbm, v_hbm, r_hbm, wg_hbm, wu_hbm, wd_hbm,
    out_ref,
    qq, kk, vv, rr, hk, hv, r_in, w_in, w_f, w_b,
    g_own, g_give, g_got, g_send0, g_send1, g_all0, g_all1,
    landz, midz, finy, landy, midy, finz, land1,
    ss_own, ss_got, attn, f_give, f_got,
    in_sem, x_send, x_recv, h_send, h_recv, gh_send, gh_recv, col_send, col_recv, fwd_send, fwd_recv,
    a_send, a_recv, b_send, b_recv, r1_send, r1_recv, y_send, y_recv, z_send, z_recv, zy_send, zy_recv,
    ss_send, ss_recv, f_send, f_recv,
):
    s = lax.axis_index("seq")
    c = lax.rem(s, 2)
    chip = s // 2
    z = lax.rem(chip, nz)
    y = chip // nz
    rows = ROWS // nz
    n_seq = ny * nz * 2
    span = y // NK
    line = y - span * NK
    partner = s + 1 - 2 * c

    def seq_at(row, column):
        return (row * nz + column) * 2 + c

    loads = [
        pltpu.make_async_copy(k_hbm, kk.at[line, c], in_sem.at[0]),
        pltpu.make_async_copy(v_hbm, vv.at[line, c], in_sem.at[1]),
        pltpu.make_async_copy(r_hbm, r_in, in_sem.at[2]),
        pltpu.make_async_copy(wg_hbm.at[0], w_in.at[0], in_sem.at[3]),
        pltpu.make_async_copy(wu_hbm.at[0], w_in.at[1], in_sem.at[4]),
        pltpu.make_async_copy(wd_hbm.at[0], w_in.at[2], in_sem.at[5]),
        pltpu.make_async_copy(q_hbm, qq.at[c], in_sem.at[6]),
    ]
    for load in loads:
        load.start()

    barrier = pltpu.get_barrier_semaphore()

    def greet(target):
        pl.semaphore_signal(barrier, inc=1, device_id={"seq": target}, device_id_type=MESH)

    for d in far_offsets(ny):
        greet(seq_at(lax.rem(y + d, ny), z))
    for d in far_offsets(nz):
        greet(seq_at(y, lax.rem(z + d, nz)))
    beside = lax.rem(s + 2 * c - 1 + n_seq, n_seq)
    greet(beside)
    greet(partner)

    for load in loads:
        load.wait()
    rr[line, c] = jnp.broadcast_to(r_in[...], (8, LANES))

    def slopes(h1, h3, dg, rate):
        sig = jax.nn.sigmoid(h1)
        s1 = h1 * sig
        a_gate = dg * h3 * sig * (1.0 + h1 * (1.0 - sig))
        return a_gate, dg * s1, (s1 * h3) * rate

    def at(m, b):
        first = (b * 3 + m) * BLOCK
        return slice(first, first + BLOCK)

    @pl.when(span == 0)
    def _():
        x, y_val = kk[line, c], vv[line, c]
        minus_r = -jnp.broadcast_to(r_in[...], (LANES, T)).T[:, 0:1]
        acts = slopes(dot_nn(x, w_in[0]), dot_nn(x, w_in[1]), dot_nn(y_val, w_in[2]) * minus_r, minus_r)
        for m in range(3):
            grad = dot_nn(acts[m].T.astype(BF16), x if m < 2 else y_val)
            low, high = grad[:HALF], grad[HALF:]
            mine = jnp.where(c == 0, low, high)
            theirs = jnp.where(c == 0, high, low).astype(BF16)
            for b in range(NL):
                for k in range(NK):
                    g_own[k, at(m, b), :] = mine[k * BLOCK:(k + 1) * BLOCK, b * LANES:(b + 1) * LANES]
                    g_give[k, at(m, b), :] = theirs[k * BLOCK:(k + 1) * BLOCK, b * LANES:(b + 1) * LANES]

    pl.semaphore_wait(barrier, ny + nz)

    def remote(src, dst, send, recv, target):
        return pltpu.make_async_remote_copy(
            src_ref=src, dst_ref=dst, send_sem=send, recv_sem=recv, device_id={"seq": target}, device_id_type=MESH
        )

    def fan(n, place, src, dst, send, recv):
        def one(i, carry):
            index, target = place(i)
            from_ref, to_ref = src(index), dst(index)

            @pl.when(target == s)
            def _():
                pltpu.make_async_copy(from_ref, to_ref, recv).start()

            @pl.when(target != s)
            def _():
                remote(from_ref, to_ref, send, recv, target).start()

            return carry

        lax.fori_loop(0, n, one, 0)

    def along_z(i):
        zt = lax.rem(z + far_first(i, nz), nz)
        return zt, seq_at(y, zt)

    def along_y(first):
        def place(i):
            k = lax.rem(line + 1 + i, NK)
            return k, seq_at(first + k, z)

        return place

    def part(column):
        return pl.ds(pl.multiple_of(column * rows, 16), rows)

    def arrived(ref, sem):
        pltpu.make_async_copy(ref, ref, sem).wait()

    def total(ref):
        out = ref[0].astype(F32)
        for i in range(1, ref.shape[0]):
            out = out + ref[i].astype(F32)
        return out.astype(BF16)

    give = remote(g_give, g_got, gh_send, gh_recv, partner)
    shares = [
        remote(ref, ref, x_send.at[i], x_recv.at[i], partner)
        for i, ref in enumerate((kk.at[line, c], vv.at[line, c], rr.at[line, c], qq.at[c]))
    ]
    halo = [
        remote(src.at[line, c], dst, h_send.at[i], h_recv.at[i], beside)
        for i, (src, dst) in enumerate(((kk, hk), (vv, hv)))
    ]
    column_of = (kk, vv, rr)

    def scatter0():
        first = y - line

        @pl.when(c == 0)
        def _():
            def send(i, carry):
                k = lax.rem(line + 1 + i, NK)
                fan(nz, along_z, lambda zt: g_send0.at[k, part(zt)], lambda zt: landz.at[k, z], a_send.at[0], a_recv.at[k])
                return carry

            lax.fori_loop(0, NK, send, 0)

        @pl.when(c == 1)
        def _():
            def send(i, carry):
                zt, _ = along_z(i)
                fan(NK, along_y(first), lambda k: g_send0.at[k, part(zt)], lambda k: landy.at[zt, line],
                    a_send.at[0], a_recv.at[zt])
                return carry

            lax.fori_loop(0, nz, send, 0)

    def scatter0_end():
        first = y - line

        @pl.when(c == 0)
        def _():
            def add(i, carry):
                k = lax.rem(line + 1 + i, NK)
                arrived(landz.at[k], a_recv.at[k])
                midz[k] = total(landz.at[k])

                @pl.when(k == line)
                def _():
                    pltpu.make_async_copy(midz.at[k], finy.at[line], b_recv).start()

                @pl.when(k != line)
                def _():
                    remote(midz.at[k], finy.at[line], b_send, b_recv, seq_at(first + k, z)).start()

                return carry

            lax.fori_loop(0, NK, add, 0)
            arrived(finy, b_recv)
            g_all0[line, part(z), :] = total(finy)

        @pl.when(c == 1)
        def _():
            def add(i, carry):
                zt, target = along_z(i)
                arrived(landy.at[zt], a_recv.at[zt])
                midy[zt] = total(landy.at[zt])

                @pl.when(zt == z)
                def _():
                    pltpu.make_async_copy(midy.at[zt], finz.at[z], b_recv).start()

                @pl.when(zt != z)
                def _():
                    remote(midy.at[zt], finz.at[z], b_send, b_recv, target).start()

                return carry

            lax.fori_loop(0, nz, add, 0)
            arrived(finz, b_recv)
            g_all0[line, part(z), :] = total(finz)

    def give_on_z(p, g_all, k):
        def one(i, carry):
            zt, target = along_z(i)
            block = g_all.at[k, part(z)]
            remote(block, block, z_send.at[p], z_recv.at[p], target).start()
            return carry

        lax.fori_loop(0, nz - 1, one, 0)

    def gather0():
        own = g_all0.at[line, part(z)]

        @pl.when(span == 0)
        def _():
            for i in range(NK):
                remote(own, own, y_send.at[0], y_recv.at[0, line], seq_at(NK + lax.rem(line + 2 + i, NK), z)).start()
            give_on_z(0, g_all0, line)
            for i in range(1, NK):
                remote(own, own, y_send.at[1], y_recv.at[0, line], seq_at(lax.rem(line + i, NK), z)).start()

        def forward(i, carry):
            k = jnp.where(span == 0, lax.rem(line + i, NK), jnp.where(y >= 6, i, NK - 1 - i))

            @pl.when((span == 1) | (k != line))
            def _():
                arrived(g_all0.at[k, part(z)], y_recv.at[0, k])
                give_on_z(0, g_all0, k)

            return carry

        lax.fori_loop(0, NK, forward, 0)

    def gather1():
        own = g_all1.at[line, part(z)]
        first = y - line

        def own_on_y(block, send, recv):
            for i in range(1, NK):
                remote(block, block, send, recv, seq_at(first + lax.rem(line + i, NK), z)).start()

        @pl.when(c == 0)
        def _():
            own_on_y(own, y_send.at[1], y_recv.at[1, line])
            give_on_z(1, g_all1, line)

            def forward(i, carry):
                k = lax.rem(line + i, NK)
                arrived(g_all1.at[k, part(z)], y_recv.at[1, k])
                give_on_z(1, g_all1, k)
                return carry

            lax.fori_loop(1, NK, forward, 0)
            arrived(g_all1.at[:, pl.ds(0, ROWS - rows)], z_recv.at[1])

        @pl.when(c == 1)
        def _():
            def one(i, carry):
                _, target = along_z(i)
                remote(own, own, zy_send.at[0], zy_recv.at[z], target).start()
                return carry

            lax.fori_loop(0, nz - 1, one, 0)
            own_on_y(own, zy_send.at[1], y_recv.at[1, 0])

            def forward(i, carry):
                zt, _ = along_z(nz - 1 - i)
                block = g_all1.at[line, part(zt)]
                arrived(block, zy_recv.at[zt])
                own_on_y(block, zy_send.at[1], y_recv.at[1, 0])
                return carry

            lax.fori_loop(1, nz, forward, 0)
            arrived(g_all1.at[pl.ds(0, NK - 1)], y_recv.at[1, 0])

    def initial_weights():
        first = pl.multiple_of(c * HALF, HALF)
        for m in range(3):
            w = w_in[m, :, pl.ds(first, HALF)].astype(F32).T
            for b in range(NL):
                for k in range(NK):
                    w_f[k, at(m, b), :] = w[k * BLOCK:(k + 1) * BLOCK, b * LANES:(b + 1) * LANES]

    def attention():
        @pl.when(c == 0)
        def _():
            for copy in halo:
                copy.wait_recv()

        @pl.when(c == 1)
        def _():
            hk[...] = kk[line, 0]
            hv[...] = vv[line, 0]

        q = qq[c]
        inv = jnp.sqrt(jnp.float32(DH))
        before = dot_nt(q, hk[...]) / inv
        here = dot_nt(q, kk[line, c]) / inv
        row = lax.broadcasted_iota(jnp.int32, (T, T), 0)
        col = lax.broadcasted_iota(jnp.int32, (T, T), 1)
        before = jnp.where((col > row) & (s > 0), before, jnp.float32(-1e30))
        here = jnp.where(col <= row, here, jnp.float32(-1e30))
        top = jnp.maximum(jnp.max(before, axis=1, keepdims=True), jnp.max(here, axis=1, keepdims=True))
        before, here = jnp.exp(before - top), jnp.exp(here - top)
        norm = jnp.sum(before, axis=1, keepdims=True) + jnp.sum(here, axis=1, keepdims=True)
        before, here = (before / norm).astype(BF16), (here / norm).astype(BF16)
        attn[...] = dot_nn(before, hv[...]) + dot_nn(here, vv[line, c])

    @pl.when(span == 0)
    def _():
        give.start()
        for share in shares:
            share.start()
        give.wait_recv()
        g_send0[...] = (g_own[...] + g_got[...].astype(F32)).astype(BF16)
        scatter0()
        initial_weights()
        for share in shares:
            share.wait_recv()
        scatter0_end()
        gather0()

        @pl.when(c == 1)
        def _():
            for copy in halo:
                copy.start()

        attention()

    @pl.when(span == 1)
    def _():
        for share in shares:
            share.start()

        @pl.when(c == 1)
        def _():
            for copy in halo:
                copy.start()

        for i in range(1, NK):
            k = lax.rem(line + i, NK)
            for j, ref in enumerate(column_of):
                own = ref.at[line, c]
                remote(own, own, col_send.at[j], col_recv.at[j, line], seq_at(NK + k, z)).start()
        initial_weights()
        for share in shares:
            share.wait_recv()
        attention()
        gather0()
        for i in range(1, NK):
            k = lax.rem(line + i, NK)
            for j, ref in enumerate(column_of):
                block = ref.at[k, c]
                arrived(block, col_recv.at[j, k])
                remote(block, block, fwd_send.at[j], fwd_recv.at[j, k], partner).start()
        for i in range(1, NK):
            k = lax.rem(line + i, NK)
            for j, ref in enumerate(column_of):
                arrived(ref.at[k, 1 - c], fwd_recv.at[j, k])

    def descend(p, g_all):
        ss_own[p] = jnp.zeros((16, LANES), F32)
        for m in range(3):
            for b in range(NL):
                g = g_all[:, at(m, b), :].astype(F32)
                ss_own[p, m * NL + b:m * NL + b + 1, :] = jnp.sum(jnp.sum(g * g, axis=0), axis=0, keepdims=True)
        swap = remote(ss_own.at[p], ss_got.at[p], ss_send.at[p], ss_recv.at[p], partner)
        swap.start()
        swap.wait()
        scale = 0.05 * lax.rsqrt((ss_own[p] + ss_got[p]) * (1.0 / FH) + 1e-06)
        for m in range(3):
            for b in range(NL):
                for k in range(NK):
                    j = m * NL + b
                    new = w_f[k, at(m, b), :] - g_all[k, at(m, b), :].astype(F32) * scale[j:j + 1]
                    w_f[k, at(m, b), :] = new
                    first = m * HALF + k * BLOCK
                    for i, term in enumerate(split(new)):
                        w_b[i, first:first + BLOCK, b * LANES:(b + 1) * LANES] = term

    arrived(g_all0.at[:, pl.ds(0, ROWS - rows)], z_recv.at[0])
    descend(0, g_all0)

    def gradient1():
        n = 2 * NK * T
        x, y_val = kk[...].reshape(n, DH), vv[...].reshape(n, DH)
        minus_r = -jnp.concatenate([rr[k, i][0:1] for k in range(NK) for i in range(2)], axis=1)

        def block(i, m):
            return w_b[i, pl.ds(pl.multiple_of(m * HALF + line * BLOCK, BLOCK), BLOCK), :]

        h = dot_nt(jnp.concatenate([block(0, 0), block(0, 1), block(1, 0), block(1, 1)], axis=0), x)
        h = h[:2 * BLOCK] + h[2 * BLOCK:]
        dg = dot_nt(jnp.concatenate([block(0, 2), block(1, 2)], axis=0), y_val)
        dg = (dg[:BLOCK] + dg[BLOCK:]) * minus_r
        a_gate, a_up, a_down = slopes(h[:BLOCK], h[BLOCK:], dg, minus_r)
        on_x = dot_nn(jnp.concatenate([a_gate, a_up], axis=0).astype(BF16), x).astype(BF16)
        on_y = dot_nn(a_down.astype(BF16), y_val).astype(BF16)
        for m, grad in enumerate((on_x[:BLOCK], on_x[BLOCK:], on_y)):
            for b in range(NL):
                g_send1[at(m, b), :] = grad[:, b * LANES:(b + 1) * LANES]

    @pl.when(span == 1)
    def _():
        gradient1()
        fan(nz, along_z, lambda zt: g_send1.at[part(zt)], lambda zt: land1.at[z], r1_send, r1_recv)
        arrived(land1, r1_recv)
        g_all1[line, part(z), :] = total(land1)
        gather1()
        descend(1, g_all1)

    def apply():
        q_all = qq[...].reshape(2 * T, DH)
        h1 = dot_nt(q_all, w_b[0, 0:HALF]) + dot_nt(q_all, w_b[1, 0:HALF])
        h3 = dot_nt(q_all, w_b[0, HALF:2 * HALF]) + dot_nt(q_all, w_b[1, HALF:2 * HALF])
        high, low = split(h1 * jax.nn.sigmoid(h1) * h3)
        w_high, w_low = w_b[0, 2 * HALF:3 * HALF], w_b[1, 2 * HALF:3 * HALF]
        f = dot_nn(high, w_high) + (dot_nn(low, w_high) + dot_nn(high, w_low))
        mine = jnp.where(c == 0, f[:T], f[T:])
        f_give[...] = jnp.where(c == 0, f[T:], f[:T])
        swap = remote(f_give, f_got, f_send, f_recv, partner)
        swap.start()
        swap.wait()
        f = mine + f_got[...]
        fast = (f * lax.rsqrt(jnp.mean(f * f, axis=1, keepdims=True) + 1e-06)).astype(BF16)
        out_ref[...] = (attn[...] + fast.astype(F32)).astype(BF16)

    apply()

    most = g_all0.at[:, pl.ds(0, ROWS - rows)]
    for share in shares:
        share.wait_send()

    @pl.when(c == 1)
    def _():
        for copy in halo:
            copy.wait_send()

    arrived(most, z_send.at[0])

    @pl.when(span == 0)
    def _():
        give.wait_send()
        arrived(landy.at[0], y_send.at[0])
        arrived(landy.at[0, pl.ds(0, NK - 1)], y_send.at[1])

        @pl.when(c == 0)
        def _():
            arrived(most, a_send.at[0])
            arrived(finy.at[pl.ds(0, NK - 1)], b_send)

        @pl.when(c == 1)
        def _():
            arrived(g_all0.at[pl.ds(0, NK - 1)], a_send.at[0])
            arrived(finz.at[pl.ds(0, nz - 1)], b_send)

    @pl.when(span == 1)
    def _():
        for j, ref in enumerate(column_of):
            arrived(ref.at[pl.ds(0, NK - 1), 0], col_send.at[j])
            arrived(ref.at[pl.ds(0, NK - 1), 0], fwd_send.at[j])
        arrived(land1.at[pl.ds(0, nz - 1)], r1_send)

        @pl.when(c == 0)
        def _():
            arrived(landy.at[0, pl.ds(0, NK - 1)], y_send.at[1])
            arrived(most, z_send.at[1])

        @pl.when(c == 1)
        def _():
            arrived(land1.at[pl.ds(0, nz - 1)], zy_send.at[0])
            arrived(g_all0.at[pl.ds(0, NK - 1)], zy_send.at[1])


def local(ny, nz, queries, keys, values, rates, gate_fast, up_fast, down_fast):
    rows = ROWS // nz
    dma = pltpu.SemaphoreType.DMA
    full = (NK, ROWS, LANES)
    return pl.pallas_call(
        functools.partial(kernel, ny, nz),
        out_shape=jax.ShapeDtypeStruct((T, DH), BF16),
        in_specs=[pl.BlockSpec(memory_space=pl.ANY)] * 7,
        out_specs=pl.BlockSpec(memory_space=pltpu.VMEM),
        scratch_shapes=[
            pltpu.VMEM((2, T, DH), BF16),
            pltpu.VMEM((NK, 2, T, DH), BF16),
            pltpu.VMEM((NK, 2, T, DH), BF16),
            pltpu.VMEM((NK, 2, 8, LANES), F32),
            pltpu.VMEM((T, DH), BF16),
            pltpu.VMEM((T, DH), BF16),
            pltpu.VMEM((1, T), F32),
            pltpu.VMEM((3, DH, FH), BF16),
            pltpu.VMEM(full, F32),
            pltpu.VMEM((2, 3 * HALF, DH), BF16),
            pltpu.VMEM(full, F32),
            pltpu.VMEM(full, BF16),
            pltpu.VMEM(full, BF16),
            pltpu.VMEM(full, BF16),
            pltpu.VMEM((ROWS, LANES), BF16),
            pltpu.VMEM(full, BF16),
            pltpu.VMEM(full, BF16),
            pltpu.VMEM((NK, nz, rows, LANES), BF16),
            pltpu.VMEM((NK, rows, LANES), BF16),
            pltpu.VMEM((NK, rows, LANES), BF16),
            pltpu.VMEM((nz, NK, rows, LANES), BF16),
            pltpu.VMEM((nz, rows, LANES), BF16),
            pltpu.VMEM((nz, rows, LANES), BF16),
            pltpu.VMEM((nz, rows, LANES), BF16),
            pltpu.VMEM((2, 16, LANES), F32),
            pltpu.VMEM((2, 16, LANES), F32),
            pltpu.VMEM((T, DH), F32),
            pltpu.VMEM((T, DH), F32),
            pltpu.VMEM((T, DH), F32),
            dma((7,)),
            dma((4,)),
            dma((4,)),
            dma((2,)),
            dma((2,)),
            dma,
            dma,
            dma((3,)),
            dma((3, NK)),
            dma((3,)),
            dma((3, NK)),
            dma((1,)),
            dma((max(NK, nz),)),
            dma,
            dma,
            dma,
            dma,
            dma((2,)),
            dma((2, NK)),
            dma((2,)),
            dma((2,)),
            dma((2,)),
            dma((nz,)),
            dma((2,)),
            dma((2,)),
            dma,
            dma,
        ],
        compiler_params=pltpu.CompilerParams(
            collective_id=0, has_side_effects=True, vmem_limit_bytes=60 * 2**20
        ),
        name="fast_layer",
    )(queries, keys, values, rates.reshape(1, T), gate_fast, up_fast, down_fast)


def solution(mesh):
    ny = 2 * NK
    nz = mesh.shape["seq"] // 2 // ny
    return jax.shard_map(
        functools.partial(local, ny, nz),
        mesh=mesh,
        in_specs=(
            P("seq", "head"),
            P("seq", "head"),
            P("seq", "head"),
            P("seq", "head"),
            P("head", None, None),
            P("head", None, None),
            P("head", None, None),
        ),
        out_specs=P("seq", "head"),
        check_vma=False,
    )
```

time: 70 us -> 65 us (0.929)
  the two profiles are of different devices: /device:TPU:61 before, /device:TPU:63 now
where the time goes in v3:
time: 65 us; the launch traced here: 64.9 us
  Pallas kernels  63.3 us (97%)
  local copies, waits for them, and re-layouts  1.57 us (2%)
    pallas_call x1, Pallas kernels, local(): pl.pallas_call(functools.partial(kernel, ny, nz), out_shape=jax.ShapeDtyp...  63.3 us
    unnamed x1, local copies, waits for them, and re-layouts  1.57 us

profile of v3, /device:TPU:63, one launch (start us, length us, event | category | flops | bytes accessed | tf_op | source)
XLA Modules:
  0.0 64.9 jit_solution(14064816823462001618)
XLA Ops:
  0.0 63.3 %fast_layer.1 = bf16[128,512]{1,0:T(8,128)(2,1)} custom-call(bf16[128,512]{1,0:T(8,128)(2,1)} %q_hbm.1, bf16[128,512]{1,0:T(8,128)(2,1)} %k_hbm.1, bf16[128,512]{1,0:T(8,128)(2,1)} %v_hbm.1, f32[1,128]{1,0:T(1,128)} %bitcast.1, bf16[1,512,256]{2,1,0:T(8,128)(2,1)} %wg_hbm.1, bf16[1,512,256]{2,1,0:T(8,128)(2,1)} %wu_hbm.1, bf16[1,512,256]{2,1,0:T(8,128)(2,1)} %wd_hbm.1), custom_call_target="tpu_custom_call" | custom-call | tf_op jit(solution)/shard_map/fast_layer/pallas_call | solution.py:529
  63.3 1.6 %copy.9 = bf16[128,512]{1,0:T(8,128)(2,1)} copy(bf16[128,512]{1,0:T(8,128)(2,1)} %fast_layer.1) | data formatting | bytes 262144

commit v4 on v3

v4 whole, which is shorter than its diff:
```python
import functools
import math

import jax
import jax.numpy as jnp
from jax import lax
from jax.experimental import pallas as pl
from jax.experimental.pallas import tpu as pltpu
from jax.sharding import PartitionSpec as P

T = 128
DH = 512
FH = 256
HALF = 128
LANES = 128
NL = DH // LANES
NK = 4
BLOCK = HALF // NK
ROWS = NL * 3 * BLOCK
MESH = pl.DeviceIdType.MESH
F32 = jnp.float32
BF16 = jnp.bfloat16


def dot_nt(a, b):
    return lax.dot_general(a, b, (((1,), (1,)), ((), ())), preferred_element_type=F32)


def dot_nn(a, b):
    return jnp.dot(a, b, preferred_element_type=F32)


def split(a):
    high = a.astype(BF16)
    return high, (a - high.astype(F32)).astype(BF16)


def far_first(j, n):
    h = (j + 1) // 2
    return lax.rem(n // 2 + n + jnp.where(lax.rem(j, 2) == 1, -h, h), n)


def far_offsets(n):
    return sorted(range(1, n), key=lambda d: -min(d, n - d))


def kernel(
    ny, nz,
    q_hbm, k_hbm, v_hbm, r_hbm, wg_hbm, wu_hbm, wd_hbm,
    out_ref,
    qq, kk, vv, rr, hk, hv, r_in, w_in, w_f, w_b,
    g_own, g_give, g_got, g_send0, g_send1, g_all0, g_all1,
    landz, midz, finy, landy, midy, finz, land1,
    ss_own, ss_got, attn, f_give, f_got,
    in_sem, x_send, x_recv, h_send, h_recv, gh_send, gh_recv, col_send, col_recv, fwd_send, fwd_recv,
    az_send, az_recv, ay_send, ay_recv, bz_send, bz_recv, by_send, by_recv, r1_send, r1_recv,
    y_send, y_recv, z_send, z_recv, zy_send, zy_recv, fy_send, fy_recv,
    ss_send, ss_recv, f_send, f_recv,
):
    s = lax.axis_index("seq")
    c = lax.rem(s, 2)
    chip = s // 2
    z = lax.rem(chip, nz)
    y = chip // nz
    rows = ROWS // nz
    n_seq = ny * nz * 2
    span = y // NK
    line = y - span * NK
    partner = s + 1 - 2 * c
    half = nz // 2
    y_first = lax.rem(z + c, 2) == 0
    up, right = lax.rem(line, 2), lax.rem(z, 2)
    group = up * 2 + right

    def seq_at(row, column):
        return (row * nz + column) * 2 + c

    loads = [
        pltpu.make_async_copy(k_hbm, kk.at[group, c], in_sem.at[0]),
        pltpu.make_async_copy(v_hbm, vv.at[group, c], in_sem.at[1]),
        pltpu.make_async_copy(r_hbm, r_in, in_sem.at[2]),
        pltpu.make_async_copy(wg_hbm.at[0], w_in.at[0], in_sem.at[3]),
        pltpu.make_async_copy(wu_hbm.at[0], w_in.at[1], in_sem.at[4]),
        pltpu.make_async_copy(wd_hbm.at[0], w_in.at[2], in_sem.at[5]),
        pltpu.make_async_copy(q_hbm, qq.at[c], in_sem.at[6]),
    ]
    for load in loads:
        load.start()

    barrier = pltpu.get_barrier_semaphore()

    def greet(target):
        pl.semaphore_signal(barrier, inc=1, device_id={"seq": target}, device_id_type=MESH)

    for d in far_offsets(ny):
        greet(seq_at(lax.rem(y + d, ny), z))
    for d in far_offsets(nz):
        greet(seq_at(y, lax.rem(z + d, nz)))
    beside = lax.rem(s + 2 * c - 1 + n_seq, n_seq)
    greet(beside)
    greet(partner)
    y_pair, z_pair = y + 1 - 2 * up, z + 1 - 2 * right
    pairs = [
        (seq_at(y_pair, z_pair), (1 - up) * 2 + 1 - right),
        (seq_at(y_pair, z), (1 - up) * 2 + right),
        (seq_at(y, z_pair), up * 2 + 1 - right),
    ]
    greet(pairs[0][0])
    other_row = y - line + lax.rem(line + 2, NK)
    for d in range(1, half):
        greet(seq_at(other_row, lax.rem(z + 2 * d, nz)))

    for load in loads:
        load.wait()
    rr[group, c] = jnp.broadcast_to(r_in[...], (8, LANES))

    def slopes(h1, h3, dg, rate):
        sig = jax.nn.sigmoid(h1)
        s1 = h1 * sig
        a_gate = dg * h3 * sig * (1.0 + h1 * (1.0 - sig))
        return a_gate, dg * s1, (s1 * h3) * rate

    def at(m, b):
        first = (b * 3 + m) * BLOCK
        return slice(first, first + BLOCK)

    @pl.when(span == 0)
    def _():
        x, y_val = kk[group, c], vv[group, c]
        minus_r = -jnp.broadcast_to(r_in[...], (LANES, T)).T[:, 0:1]
        acts = slopes(dot_nn(x, w_in[0]), dot_nn(x, w_in[1]), dot_nn(y_val, w_in[2]) * minus_r, minus_r)
        for m in range(3):
            grad = dot_nn(acts[m].T.astype(BF16), x if m < 2 else y_val)
            low, high = grad[:HALF], grad[HALF:]
            mine = jnp.where(c == 0, low, high)
            theirs = jnp.where(c == 0, high, low).astype(BF16)
            for b in range(NL):
                for k in range(NK):
                    g_own[k, at(m, b), :] = mine[k * BLOCK:(k + 1) * BLOCK, b * LANES:(b + 1) * LANES]
                    g_give[k, at(m, b), :] = theirs[k * BLOCK:(k + 1) * BLOCK, b * LANES:(b + 1) * LANES]

    pl.semaphore_wait(barrier, ny + nz + half)

    def remote(src, dst, send, recv, target):
        return pltpu.make_async_remote_copy(
            src_ref=src, dst_ref=dst, send_sem=send, recv_sem=recv, device_id={"seq": target}, device_id_type=MESH
        )

    def fan(n, place, src, dst, send, recv):
        def one(i, carry):
            index, target = place(i)
            from_ref, to_ref = src(index), dst(index)

            @pl.when(target == s)
            def _():
                pltpu.make_async_copy(from_ref, to_ref, recv).start()

            @pl.when(target != s)
            def _():
                remote(from_ref, to_ref, send, recv, target).start()

            return carry

        lax.fori_loop(0, n, one, 0)

    def along_z(i):
        zt = lax.rem(z + far_first(i, nz), nz)
        return zt, seq_at(y, zt)

    def column(i, kind):
        return 2 * lax.rem(z // 2 + far_first(i, half), half) + (c if kind == 0 else 1 - c)

    def row(i):
        return lax.rem(line + i, NK)

    def part(i):
        return pl.ds(pl.multiple_of(i * rows, 16), rows)

    def arrived(ref, sem):
        pltpu.make_async_copy(ref, ref, sem).wait()

    def total(ref):
        out = ref[0].astype(F32)
        for i in range(1, ref.shape[0]):
            out = out + ref[i].astype(F32)
        return out.astype(BF16)

    give = remote(g_give, g_got, gh_send, gh_recv, partner)
    shares = [
        remote(ref, ref, x_send.at[i], x_recv.at[i], partner)
        for i, ref in enumerate((kk.at[group, c], vv.at[group, c], rr.at[group, c], qq.at[c]))
    ]
    halo = [
        remote(src.at[group, c], dst, h_send.at[i], h_recv.at[i], beside)
        for i, (src, dst) in enumerate(((kk, hk), (vv, hv)))
    ]
    group_of = (kk, vv, rr)

    def scatter0():
        first = y - line

        def send(i, carry):
            k = row(i + 1)

            def place_z(j):
                zt = column(j, 0)
                return zt, seq_at(y, zt)

            fan(half, place_z, lambda zt: g_send0.at[k, part(zt)], lambda zt: landz.at[k, z], az_send, az_recv.at[k])
            return carry

        def send_y(i, carry):
            zt = column(i, 1)

            def place_y(j):
                k = row(j + 1)
                return k, seq_at(first + k, z)

            fan(NK, place_y, lambda k: g_send0.at[k, part(zt)], lambda k: landy.at[zt // 2, line], ay_send, ay_recv.at[zt // 2])
            return carry

        for i in range(max(NK, half)):
            if i < NK:
                send(i, 0)
            if i < half:
                send_y(i, 0)

    def scatter0_end():
        first = y - line

        def add_z(i):
            k = row(i + 1)
            arrived(landz.at[k], az_recv.at[k])
            midz[k] = total(landz.at[k])

            @pl.when(k == line)
            def _():
                pltpu.make_async_copy(midz.at[k], finy.at[line], by_recv).start()

            @pl.when(k != line)
            def _():
                remote(midz.at[k], finy.at[line], by_send, by_recv, seq_at(first + k, z)).start()

        def add_y(i):
            zt = column(i, 1)
            j = zt // 2
            arrived(landy.at[j], ay_recv.at[j])
            midy[j] = total(landy.at[j])

            @pl.when(zt == z)
            def _():
                pltpu.make_async_copy(midy.at[j], finz.at[z], bz_recv).start()

            @pl.when(zt != z)
            def _():
                remote(midy.at[j], finz.at[z], bz_send, bz_recv, seq_at(y, zt)).start()

        for i in range(max(NK, half)):
            if i < half:
                add_y(i)
            if i < NK:

                @pl.when(y_first)
                def _():
                    add_z(i)

        @pl.when(y_first)
        def _():
            arrived(finy, by_recv)
            g_all0[line, part(z), :] = total(finy)

        @pl.when(jnp.logical_not(y_first))
        def _():
            arrived(finz, bz_recv)
            g_all0[line, part(z), :] = total(finz)

    def to_z(block, send, recv):
        def one(i, carry):
            _, target = along_z(i)
            remote(block, block, send, recv, target).start()
            return carry

        lax.fori_loop(0, nz - 1, one, 0)

    def to_own_span(block, send, recv):
        for i in range(1, NK):
            remote(block, block, send, recv, seq_at(y - line + row(i), z)).start()

    def to_span1(block, send, recv):
        for i in range(NK):
            remote(block, block, send, recv, seq_at(NK + row(i + 2), z)).start()

    def gather0():
        def block(k, zt):
            return g_all0.at[k, part(zt)]

        own = block(line, z)

        def forward_z(k):
            arrived(block(k, z), y_recv.at[0, k])
            to_z(block(k, z), z_send.at[0], z_recv.at[0])

        @pl.when(span == 0)
        def _():
            @pl.when(y_first)
            def _():
                to_span1(own, y_send.at[0], y_recv.at[0, line])
                to_own_span(own, y_send.at[1], y_recv.at[0, line])

            @pl.when(jnp.logical_not(y_first))
            def _():
                to_z(own, zy_send.at[0], zy_recv.at[0, z])
                to_span1(own, fy_send.at[0], fy_recv.at[0])

            for i in range(half):
                zt = column(half - 1 - i, 1)

                @pl.when(zt != z)
                def _():
                    arrived(block(line, zt), zy_recv.at[0, zt])
                    to_span1(block(line, zt), fy_send.at[0], fy_recv.at[0])

            for i in range(half):
                to_own_span(block(line, column(i, 1)), fy_send.at[1], fy_recv.at[0])

            @pl.when(y_first)
            def _():
                to_z(own, z_send.at[0], z_recv.at[0])
                for i in range(1, NK):
                    forward_z(row(i))

        @pl.when((span == 1) & y_first)
        def _():
            for i in range(NK):
                forward_z(jnp.where(line >= 2, i, NK - 1 - i))

    def gathered(p):
        @pl.when(y_first)
        def _():
            arrived(landz.at[:, pl.ds(0, half - 1)], z_recv.at[p])

        @pl.when(jnp.logical_not(y_first))
        def _():
            arrived(landz.at[:, pl.ds(0, half)], z_recv.at[p])

    def place1(k, zt):
        return g_all1.at[lax.rem(k, 2) * 2 + lax.rem(zt, 2), part(k // 2 * half + zt // 2)]

    def gather1():
        own = place1(line, z)

        @pl.when(y_first)
        def _():
            to_own_span(own, y_send.at[0], y_recv.at[1, line])
            to_z(own, z_send.at[1], z_recv.at[1])

        @pl.when(jnp.logical_not(y_first))
        def _():
            to_z(own, zy_send.at[1], zy_recv.at[1, z])
            to_own_span(own, fy_send.at[0], fy_recv.at[1])

        for i in range(max(NK, half)):
            if i < half:
                zt = column(half - 1 - i, 1)

                @pl.when(zt != z)
                def _():
                    arrived(place1(line, zt), zy_recv.at[1, zt])
                    to_own_span(place1(line, zt), fy_send.at[0], fy_recv.at[1])

            if 1 <= i < NK:

                @pl.when(y_first)
                def _():
                    k = row(i)
                    arrived(place1(k, z), y_recv.at[1, k])
                    to_z(place1(k, z), z_send.at[1], z_recv.at[1])

    def initial_weights():
        first = pl.multiple_of(c * HALF, HALF)
        for m in range(3):
            w = w_in[m, :, pl.ds(first, HALF)].astype(F32).T
            for b in range(NL):
                for k in range(NK):
                    w_f[k, at(m, b), :] = w[k * BLOCK:(k + 1) * BLOCK, b * LANES:(b + 1) * LANES]

    def attention():
        @pl.when(c == 0)
        def _():
            for copy in halo:
                copy.wait_recv()

        @pl.when(c == 1)
        def _():
            hk[...] = kk[group, 0]
            hv[...] = vv[group, 0]

        q = qq[c]
        inv = jnp.sqrt(jnp.float32(DH))
        before = dot_nt(q, hk[...]) / inv
        here = dot_nt(q, kk[group, c]) / inv
        t_q = lax.broadcasted_iota(jnp.int32, (T, T), 0)
        t_k = lax.broadcasted_iota(jnp.int32, (T, T), 1)
        before = jnp.where((t_k > t_q) & (s > 0), before, jnp.float32(-1e30))
        here = jnp.where(t_k <= t_q, here, jnp.float32(-1e30))
        top = jnp.maximum(jnp.max(before, axis=1, keepdims=True), jnp.max(here, axis=1, keepdims=True))
        before, here = jnp.exp(before - top), jnp.exp(here - top)
        norm = jnp.sum(before, axis=1, keepdims=True) + jnp.sum(here, axis=1, keepdims=True)
        before, here = (before / norm).astype(BF16), (here / norm).astype(BF16)
        attn[...] = dot_nn(before, hv[...]) + dot_nn(here, vv[group, c])

    last_chip = chip == NK * nz - 1

    def start_halo():
        for copy in halo:
            copy.start()

    @pl.when(span == 0)
    def _():
        give.start()
        for share in shares:
            share.start()
        pl.when((c == 1) & last_chip)(start_halo)
        give.wait_recv()
        g_send0[...] = (g_own[...] + g_got[...].astype(F32)).astype(BF16)
        scatter0()
        initial_weights()
        for share in shares:
            share.wait_recv()
        scatter0_end()
        gather0()
        pl.when((c == 1) & jnp.logical_not(last_chip))(start_halo)
        attention()
        arrived(landy.at[:, pl.ds(0, NK - 1)], fy_recv.at[0])

    @pl.when(span == 1)
    def _():
        for share in shares:
            share.start()
        pl.when(c == 1)(start_halo)
        for target, _ in pairs:
            for j, ref in enumerate(group_of):
                own = ref.at[group, c]
                remote(own, own, col_send.at[j], col_recv.at[j, group], target).start()
        initial_weights()
        for share in shares:
            share.wait_recv()
        attention()
        for _, k in pairs:
            for j, ref in enumerate(group_of):
                block = ref.at[k, c]
                arrived(block, col_recv.at[j, k])
                remote(block, block, fwd_send.at[j], fwd_recv.at[j, k], partner).start()
        gather0()
        for _, k in pairs:
            for j, ref in enumerate(group_of):
                arrived(ref.at[k, 1 - c], fwd_recv.at[j, k])
        arrived(landy, fy_recv.at[0])

    def descend(p, g_all):
        ss_own[p] = jnp.zeros((16, LANES), F32)
        for m in range(3):
            for b in range(NL):
                g = g_all[:, at(m, b), :].astype(F32)
                ss_own[p, m * NL + b:m * NL + b + 1, :] = jnp.sum(jnp.sum(g * g, axis=0), axis=0, keepdims=True)
        swap = remote(ss_own.at[p], ss_got.at[p], ss_send.at[p], ss_recv.at[p], partner)
        swap.start()
        swap.wait()
        scale = 0.05 * lax.rsqrt((ss_own[p] + ss_got[p]) * (1.0 / FH) + 1e-06)
        for m in range(3):
            for b in range(NL):
                for k in range(NK):
                    j = m * NL + b
                    new = w_f[k, at(m, b), :] - g_all[k, at(m, b), :].astype(F32) * scale[j:j + 1]
                    w_f[k, at(m, b), :] = new
                    first = m * HALF + k * BLOCK
                    for i, term in enumerate(split(new)):
                        w_b[i, first:first + BLOCK, b * LANES:(b + 1) * LANES] = term

    gathered(0)
    descend(0, g_all0)

    def gradient1():
        n = 2 * NK * T
        x, y_val = kk[...].reshape(n, DH), vv[...].reshape(n, DH)
        minus_r = -jnp.concatenate([rr[k, i][0:1] for k in range(NK) for i in range(2)], axis=1)

        def block(i, m):
            return w_b[i, pl.ds(pl.multiple_of(m * HALF + group * BLOCK, BLOCK), BLOCK), :]

        h = dot_nt(jnp.concatenate([block(0, 0), block(0, 1), block(1, 0), block(1, 1)], axis=0), x)
        h = h[:2 * BLOCK] + h[2 * BLOCK:]
        dg = dot_nt(jnp.concatenate([block(0, 2), block(1, 2)], axis=0), y_val)
        dg = (dg[:BLOCK] + dg[BLOCK:]) * minus_r
        a_gate, a_up, a_down = slopes(h[:BLOCK], h[BLOCK:], dg, minus_r)
        on_x = dot_nn(jnp.concatenate([a_gate, a_up], axis=0).astype(BF16), x).astype(BF16)
        on_y = dot_nn(a_down.astype(BF16), y_val).astype(BF16)
        for m, grad in enumerate((on_x[:BLOCK], on_x[BLOCK:], on_y)):
            for b in range(NL):
                g_send1[at(m, b), :] = grad[:, b * LANES:(b + 1) * LANES]

    @pl.when(span == 1)
    def _():
        gradient1()

        def counterpart(i):
            k = lax.rem(line + 2 - 2 * lax.rem(i, 2), NK)
            zt = 2 * lax.rem(z // 2 + far_first(i // 2, half), half) + right
            return k // 2 * half + zt // 2, seq_at(NK + k, zt)

        mine = line // 2 * half + z // 2
        fan(nz, counterpart, lambda i: g_send1.at[part(i)], lambda i: land1.at[mine], r1_send, r1_recv)
        arrived(land1, r1_recv)
        g_all1[group, part(mine), :] = total(land1)
        gather1()
        arrived(landy.at[:, pl.ds(0, NK - 1)], fy_recv.at[1])
        gathered(1)
        descend(1, g_all1)

    def apply():
        q_all = qq[...].reshape(2 * T, DH)
        h1 = dot_nt(q_all, w_b[0, 0:HALF]) + dot_nt(q_all, w_b[1, 0:HALF])
        h3 = dot_nt(q_all, w_b[0, HALF:2 * HALF]) + dot_nt(q_all, w_b[1, HALF:2 * HALF])
        high, low = split(h1 * jax.nn.sigmoid(h1) * h3)
        w_high, w_low = w_b[0, 2 * HALF:3 * HALF], w_b[1, 2 * HALF:3 * HALF]
        f = dot_nn(high, w_high) + (dot_nn(low, w_high) + dot_nn(high, w_low))
        mine = jnp.where(c == 0, f[:T], f[T:])
        f_give[...] = jnp.where(c == 0, f[T:], f[:T])
        swap = remote(f_give, f_got, f_send, f_recv, partner)
        swap.start()
        swap.wait()
        f = mine + f_got[...]
        fast = (f * lax.rsqrt(jnp.mean(f * f, axis=1, keepdims=True) + 1e-06)).astype(BF16)
        out_ref[...] = (attn[...] + fast.astype(F32)).astype(BF16)

    apply()

    def left(whole, sem, one_stayed):
        @pl.when(one_stayed)
        def _():
            arrived(whole(1), sem)

        @pl.when(jnp.logical_not(one_stayed))
        def _():
            arrived(whole(0), sem)

    most = g_all0.at[:, pl.ds(0, ROWS - rows)]
    three = finy.at[pl.ds(0, NK - 1)]
    z_first = jnp.logical_not(y_first)
    for share in shares:
        share.wait_send()

    @pl.when(c == 1)
    def _():
        for copy in halo:
            copy.wait_send()

    @pl.when(y_first)
    def _():
        arrived(most, z_send.at[0])

    @pl.when(span == 0)
    def _():
        give.wait_send()
        left(lambda n: landz.at[:, pl.ds(0, half - n)], az_send, y_first)
        arrived(landy.at[:, pl.ds(0, NK - 1)], ay_send)
        left(lambda n: finz.at[pl.ds(0, half - n)], bz_send, z_first)
        arrived(landy, fy_send.at[0])
        arrived(landy.at[:, pl.ds(0, NK - 1)], fy_send.at[1])

        @pl.when(y_first)
        def _():
            arrived(three, by_send)
            arrived(finy, y_send.at[0])
            arrived(three, y_send.at[1])

        @pl.when(z_first)
        def _():
            arrived(finz.at[pl.ds(0, nz - 1)], zy_send.at[0])

    @pl.when(span == 1)
    def _():
        for j, ref in enumerate(group_of):
            arrived(ref.at[pl.ds(0, 3), 0], col_send.at[j])
            arrived(ref.at[pl.ds(0, 3), 0], fwd_send.at[j])
        arrived(land1.at[pl.ds(0, nz - 1)], r1_send)
        arrived(landy.at[:, pl.ds(0, NK - 1)], fy_send.at[0])

        @pl.when(y_first)
        def _():
            arrived(three, y_send.at[0])
            arrived(most, z_send.at[1])

        @pl.when(z_first)
        def _():
            arrived(finz.at[pl.ds(0, nz - 1)], zy_send.at[1])


def local(ny, nz, queries, keys, values, rates, gate_fast, up_fast, down_fast):
    rows = ROWS // nz
    dma = pltpu.SemaphoreType.DMA
    full = (NK, ROWS, LANES)
    return pl.pallas_call(
        functools.partial(kernel, ny, nz),
        out_shape=jax.ShapeDtypeStruct((T, DH), BF16),
        in_specs=[pl.BlockSpec(memory_space=pl.ANY)] * 7,
        out_specs=pl.BlockSpec(memory_space=pltpu.VMEM),
        scratch_shapes=[
            pltpu.VMEM((2, T, DH), BF16),
            pltpu.VMEM((NK, 2, T, DH), BF16),
            pltpu.VMEM((NK, 2, T, DH), BF16),
            pltpu.VMEM((NK, 2, 8, LANES), F32),
            pltpu.VMEM((T, DH), BF16),
            pltpu.VMEM((T, DH), BF16),
            pltpu.VMEM((1, T), F32),
            pltpu.VMEM((3, DH, FH), BF16),
            pltpu.VMEM(full, F32),
            pltpu.VMEM((2, 3 * HALF, DH), BF16),
            pltpu.VMEM(full, F32),
            pltpu.VMEM(full, BF16),
            pltpu.VMEM(full, BF16),
            pltpu.VMEM(full, BF16),
            pltpu.VMEM((ROWS, LANES), BF16),
            pltpu.VMEM(full, BF16),
            pltpu.VMEM(full, BF16),
            pltpu.VMEM((NK, nz, rows, LANES), BF16),
            pltpu.VMEM((NK, rows, LANES), BF16),
            pltpu.VMEM((NK, rows, LANES), BF16),
            pltpu.VMEM((nz // 2, NK, rows, LANES), BF16),
            pltpu.VMEM((nz // 2, rows, LANES), BF16),
            pltpu.VMEM((nz, rows, LANES), BF16),
            pltpu.VMEM((nz, rows, LANES), BF16),
            pltpu.VMEM((2, 16, LANES), F32),
            pltpu.VMEM((2, 16, LANES), F32),
            pltpu.VMEM((T, DH), F32),
            pltpu.VMEM((T, DH), F32),
            pltpu.VMEM((T, DH), F32),
            dma((7,)),
            dma((4,)),
            dma((4,)),
            dma((2,)),
            dma((2,)),
            dma,
            dma,
            dma((3,)),
            dma((3, NK)),
            dma((3,)),
            dma((3, NK)),
            dma,
            dma((NK,)),
            dma,
            dma((nz // 2,)),
            dma,
            dma,
            dma,
            dma,
            dma,
            dma,
            dma((2,)),
            dma((2, NK)),
            dma((2,)),
            dma((2,)),
            dma((2,)),
            dma((2, nz)),
            dma((2,)),
            dma((2,)),
            dma((2,)),
            dma((2,)),
            dma,
            dma,
        ],
        compiler_params=pltpu.CompilerParams(
            collective_id=0, has_side_effects=True, vmem_limit_bytes=60 * 2**20
        ),
        name="fast_layer",
    )(queries, keys, values, rates.reshape(1, T), gate_fast, up_fast, down_fast)


def solution(mesh):
    ny = 2 * NK
    nz = mesh.shape["seq"] // 2 // ny
    return jax.shard_map(
        functools.partial(local, ny, nz),
        mesh=mesh,
        in_specs=(
            P("seq", "head"),
            P("seq", "head"),
            P("seq", "head"),
            P("seq", "head"),
            P("head", None, None),
            P("head", None, None),
            P("head", None, None),
        ),
        out_specs=P("seq", "head"),
        check_vma=False,
    )
```

time: 65 us -> 63.8 us (0.982)
  the two profiles are of different devices: /device:TPU:63 before, /device:TPU:49 now
where the time goes in v4:
time: 63.8 us; the launch traced here: 63.7 us
  Pallas kernels  62.1 us (97%)
  local copies, waits for them, and re-layouts  1.57 us (2%)
    pallas_call x1, Pallas kernels, local(): pl.pallas_call(functools.partial(kernel, ny, nz), out_shape=jax.ShapeDtyp...  62.1 us
    unnamed x1, local copies, waits for them, and re-layouts  1.57 us

profile of v4, /device:TPU:49, one launch (start us, length us, event | category | flops | bytes accessed | tf_op | source)
XLA Modules:
  0.0 63.7 jit_solution(14913180173831557738)
XLA Ops:
  0.0 62.1 %fast_layer.1 = bf16[128,512]{1,0:T(8,128)(2,1)} custom-call(bf16[128,512]{1,0:T(8,128)(2,1)} %q_hbm.1, bf16[128,512]{1,0:T(8,128)(2,1)} %k_hbm.1, bf16[128,512]{1,0:T(8,128)(2,1)} %v_hbm.1, f32[1,128]{1,0:T(1,128)} %bitcast.1, bf16[1,512,256]{2,1,0:T(8,128)(2,1)} %wg_hbm.1, bf16[1,512,256]{2,1,0:T(8,128)(2,1)} %wu_hbm.1, bf16[1,512,256]{2,1,0:T(8,128)(2,1)} %wd_hbm.1), custom_call_target="tpu_custom_call" | custom-call | tf_op jit(solution)/shard_map/fast_layer/pallas_call | solution.py:603
  62.1 1.6 %copy.9 = bf16[128,512]{1,0:T(8,128)(2,1)} copy(bf16[128,512]{1,0:T(8,128)(2,1)} %fast_layer.1) | data formatting | bytes 262144

commit v5 on v4

--- a/solution.py
+++ b/solution.py
@@ -69,6 +69,8 @@
     partner = s + 1 - 2 * c
     half = nz // 2
     y_first = lax.rem(z + c, 2) == 0
+    fourth = nz // 4
+    y_first0 = lax.rem(z + 2 * c, 4) != 3
     up, right = lax.rem(line, 2), lax.rem(z, 2)
     group = up * 2 + right
 
@@ -294,6 +296,9 @@
         def block(k, zt):
             return g_all0.at[k, part(zt)]
 
+        def column0(i):
+            return 4 * lax.rem(z // 4 + i, fourth) + 3 - 2 * c
+
         own = block(line, z)
 
         def forward_z(k):
@@ -302,46 +307,46 @@
 
         @pl.when(span == 0)
         def _():
-            @pl.when(y_first)
+            @pl.when(y_first0)
             def _():
                 to_span1(own, y_send.at[0], y_recv.at[0, line])
                 to_own_span(own, y_send.at[1], y_recv.at[0, line])
 
-            @pl.when(jnp.logical_not(y_first))
+            @pl.when(jnp.logical_not(y_first0))
             def _():
                 to_z(own, zy_send.at[0], zy_recv.at[0, z])
                 to_span1(own, fy_send.at[0], fy_recv.at[0])
 
-            for i in range(half):
-                zt = column(half - 1 - i, 1)
+            for i in range(fourth):
+                zt = column0(i)
 
                 @pl.when(zt != z)
                 def _():
                     arrived(block(line, zt), zy_recv.at[0, zt])
                     to_span1(block(line, zt), fy_send.at[0], fy_recv.at[0])
 
-            for i in range(half):
-                to_own_span(block(line, column(i, 1)), fy_send.at[1], fy_recv.at[0])
-
-            @pl.when(y_first)
+            for i in range(fourth):
+                to_own_span(block(line, column0(i)), fy_send.at[1], fy_recv.at[0])
+
+            @pl.when(y_first0)
             def _():
                 to_z(own, z_send.at[0], z_recv.at[0])
                 for i in range(1, NK):
                     forward_z(row(i))
 
-        @pl.when((span == 1) & y_first)
+        @pl.when((span == 1) & y_first0)
         def _():
             for i in range(NK):
                 forward_z(jnp.where(line >= 2, i, NK - 1 - i))
 
-    def gathered(p):
-        @pl.when(y_first)
-        def _():
-            arrived(landz.at[:, pl.ds(0, half - 1)], z_recv.at[p])
-
-        @pl.when(jnp.logical_not(y_first))
-        def _():
-            arrived(landz.at[:, pl.ds(0, half)], z_recv.at[p])
+    def gathered(p, along_y_first, columns):
+        @pl.when(along_y_first)
+        def _():
+            arrived(landz.at[:, pl.ds(0, columns - 1)], z_recv.at[p])
+
+        @pl.when(jnp.logical_not(along_y_first))
+        def _():
+            arrived(landz.at[:, pl.ds(0, columns)], z_recv.at[p])
 
     def place1(k, zt):
         return g_all1.at[lax.rem(k, 2) * 2 + lax.rem(zt, 2), part(k // 2 * half + zt // 2)]
@@ -431,7 +436,7 @@
         gather0()
         pl.when((c == 1) & jnp.logical_not(last_chip))(start_halo)
         attention()
-        arrived(landy.at[:, pl.ds(0, NK - 1)], fy_recv.at[0])
+        arrived(landy.at[pl.ds(0, fourth), pl.ds(0, NK - 1)], fy_recv.at[0])
 
     @pl.when(span == 1)
     def _():
@@ -443,21 +448,21 @@
                 own = ref.at[group, c]
                 remote(own, own, col_send.at[j], col_recv.at[j, group], target).start()
         initial_weights()
+        gather0()
+        for _, k in pairs:
+            for j, ref in enumerate(group_of):
+                block = ref.at[k, c]
+                arrived(block, col_recv.at[j, k])
+                remote(block, block, fwd_send.at[j], fwd_recv.at[j, k], partner).start()
         for share in shares:
             share.wait_recv()
         attention()
         for _, k in pairs:
             for j, ref in enumerate(group_of):
-                block = ref.at[k, c]
-                arrived(block, col_recv.at[j, k])
-                remote(block, block, fwd_send.at[j], fwd_recv.at[j, k], partner).start()
-        gather0()
-        for _, k in pairs:
-            for j, ref in enumerate(group_of):
                 arrived(ref.at[k, 1 - c], fwd_recv.at[j, k])
-        arrived(landy, fy_recv.at[0])
-
-    def descend(p, g_all):
+        arrived(landy.at[pl.ds(0, fourth)], fy_recv.at[0])
+
+    def row_scales(p, g_all):
         ss_own[p] = jnp.zeros((16, LANES), F32)
         for m in range(3):
             for b in range(NL):
@@ -466,19 +471,26 @@
         swap = remote(ss_own.at[p], ss_got.at[p], ss_send.at[p], ss_recv.at[p], partner)
         swap.start()
         swap.wait()
+
+    def descend(p, g_all, blocks):
         scale = 0.05 * lax.rsqrt((ss_own[p] + ss_got[p]) * (1.0 / FH) + 1e-06)
-        for m in range(3):
-            for b in range(NL):
-                for k in range(NK):
+        for k in blocks:
+            for m in range(3):
+                for b in range(NL):
                     j = m * NL + b
                     new = w_f[k, at(m, b), :] - g_all[k, at(m, b), :].astype(F32) * scale[j:j + 1]
                     w_f[k, at(m, b), :] = new
                     first = m * HALF + k * BLOCK
+                    place = slice(first, first + BLOCK) if isinstance(k, int) else pl.ds(pl.multiple_of(first, BLOCK), BLOCK)
                     for i, term in enumerate(split(new)):
-                        w_b[i, first:first + BLOCK, b * LANES:(b + 1) * LANES] = term
-
-    gathered(0)
-    descend(0, g_all0)
+                        w_b[i, place, b * LANES:(b + 1) * LANES] = term
+
+    gathered(0, y_first0, nz - fourth)
+    row_scales(0, g_all0)
+
+    @pl.when(span == 0)
+    def _():
+        descend(0, g_all0, range(NK))
 
     def gradient1():
         n = 2 * NK * T
@@ -501,6 +513,7 @@
 
     @pl.when(span == 1)
     def _():
+        descend(0, g_all0, [group])
         gradient1()
 
         def counterpart(i):
@@ -510,24 +523,27 @@
 
         mine = line // 2 * half + z // 2
         fan(nz, counterpart, lambda i: g_send1.at[part(i)], lambda i: land1.at[mine], r1_send, r1_recv)
+        descend(0, g_all0, [lax.rem(group + i, NK) for i in range(1, NK)])
         arrived(land1, r1_recv)
         g_all1[group, part(mine), :] = total(land1)
         gather1()
         arrived(landy.at[:, pl.ds(0, NK - 1)], fy_recv.at[1])
-        gathered(1)
-        descend(1, g_all1)
+        gathered(1, y_first, half)
+        row_scales(1, g_all1)
+        descend(1, g_all1, range(NK))
 
     def apply():
-        q_all = qq[...].reshape(2 * T, DH)
-        h1 = dot_nt(q_all, w_b[0, 0:HALF]) + dot_nt(q_all, w_b[1, 0:HALF])
-        h3 = dot_nt(q_all, w_b[0, HALF:2 * HALF]) + dot_nt(q_all, w_b[1, HALF:2 * HALF])
-        high, low = split(h1 * jax.nn.sigmoid(h1) * h3)
-        w_high, w_low = w_b[0, 2 * HALF:3 * HALF], w_b[1, 2 * HALF:3 * HALF]
-        f = dot_nn(high, w_high) + (dot_nn(low, w_high) + dot_nn(high, w_low))
-        mine = jnp.where(c == 0, f[:T], f[T:])
-        f_give[...] = jnp.where(c == 0, f[T:], f[:T])
+        def half_sum(q):
+            h1 = dot_nt(q, w_b[0, 0:HALF]) + dot_nt(q, w_b[1, 0:HALF])
+            h3 = dot_nt(q, w_b[0, HALF:2 * HALF]) + dot_nt(q, w_b[1, HALF:2 * HALF])
+            high, low = split(h1 * jax.nn.sigmoid(h1) * h3)
+            w_high, w_low = w_b[0, 2 * HALF:3 * HALF], w_b[1, 2 * HALF:3 * HALF]
+            return dot_nn(high, w_high) + (dot_nn(low, w_high) + dot_nn(high, w_low))
+
+        f_give[...] = half_sum(qq[1 - c])
         swap = remote(f_give, f_got, f_send, f_recv, partner)
         swap.start()
+        mine = half_sum(qq[c])
         swap.wait()
         f = mine + f_got[...]
         fast = (f * lax.rsqrt(jnp.mean(f * f, axis=1, keepdims=True) + 1e-06)).astype(BF16)
@@ -555,7 +571,7 @@
         for copy in halo:
             copy.wait_send()
 
-    @pl.when(y_first)
+    @pl.when(y_first0)
     def _():
         arrived(most, z_send.at[0])
 
@@ -565,16 +581,19 @@
         left(lambda n: landz.at[:, pl.ds(0, half - n)], az_send, y_first)
         arrived(landy.at[:, pl.ds(0, NK - 1)], ay_send)
         left(lambda n: finz.at[pl.ds(0, half - n)], bz_send, z_first)
-        arrived(landy, fy_send.at[0])
-        arrived(landy.at[:, pl.ds(0, NK - 1)], fy_send.at[1])
+        arrived(landy.at[pl.ds(0, fourth)], fy_send.at[0])
+        arrived(landy.at[pl.ds(0, fourth), pl.ds(0, NK - 1)], fy_send.at[1])
 
         @pl.when(y_first)
         def _():
             arrived(three, by_send)
+
+        @pl.when(y_first0)
+        def _():
             arrived(finy, y_send.at[0])
             arrived(three, y_send.at[1])
 
-        @pl.when(z_first)
+        @pl.when(jnp.logical_not(y_first0))
         def _():
             arrived(finz.at[pl.ds(0, nz - 1)], zy_send.at[0])
 

time: 63.8 us -> 63.1 us (0.989)
  the two profiles are of different devices: /device:TPU:49 before, /device:TPU:51 now
where the time goes in v5:
time: 63.1 us; the launch traced here: 63 us
  Pallas kernels  61.4 us (97%)
  local copies, waits for them, and re-layouts  1.57 us (2%)
    pallas_call x1, Pallas kernels, local(): pl.pallas_call(functools.partial(kernel, ny, nz), out_shape=jax.ShapeDtyp...  61.4 us
    unnamed x1, local copies, waits for them, and re-layouts  1.57 us

profile of v5, /device:TPU:51, one launch (start us, length us, event | category | flops | bytes accessed | tf_op | source)
XLA Modules:
  0.0 63.0 jit_solution(4432570134616495921)
XLA Ops:
  0.0 61.4 %fast_layer.1 = bf16[128,512]{1,0:T(8,128)(2,1)} custom-call(bf16[128,512]{1,0:T(8,128)(2,1)} %q_hbm.1, bf16[128,512]{1,0:T(8,128)(2,1)} %k_hbm.1, bf16[128,512]{1,0:T(8,128)(2,1)} %v_hbm.1, f32[1,128]{1,0:T(1,128)} %bitcast.1, bf16[1,512,256]{2,1,0:T(8,128)(2,1)} %wg_hbm.1, bf16[1,512,256]{2,1,0:T(8,128)(2,1)} %wu_hbm.1, bf16[1,512,256]{2,1,0:T(8,128)(2,1)} %wd_hbm.1), custom_call_target="tpu_custom_call" | custom-call | tf_op jit(solution)/shard_map/fast_layer/pallas_call | solution.py:622
  61.4 1.6 %copy.9 = bf16[128,512]{1,0:T(8,128)(2,1)} copy(bf16[128,512]{1,0:T(8,128)(2,1)} %fast_layer.1) | data formatting | bytes 262144

commit v6 on v5

--- a/solution.py
+++ b/solution.py
@@ -50,10 +50,10 @@
     out_ref,
     qq, kk, vv, rr, hk, hv, r_in, w_in, w_f, w_b,
     g_own, g_give, g_got, g_send0, g_send1, g_all0, g_all1,
-    landz, midz, finy, landy, midy, finz, land1,
+    landz, midz, landp, finy, landy, midy, finz, land1,
     ss_own, ss_got, attn, f_give, f_got,
     in_sem, x_send, x_recv, h_send, h_recv, gh_send, gh_recv, col_send, col_recv, fwd_send, fwd_recv,
-    az_send, az_recv, ay_send, ay_recv, bz_send, bz_recv, by_send, by_recv, r1_send, r1_recv,
+    az_send, az_recv, ay_send, ay_recv, bz_send, bz_recv, p_send, p_recv, r1_send, r1_recv,
     y_send, y_recv, z_send, z_recv, zy_send, zy_recv, fy_send, fy_recv,
     ss_send, ss_recv, f_send, f_recv,
 ):
@@ -70,7 +70,7 @@
     half = nz // 2
     y_first = lax.rem(z + c, 2) == 0
     fourth = nz // 4
-    y_first0 = lax.rem(z + 2 * c, 4) != 3
+    y_first0 = lax.rem(z + c, 4) != 3
     up, right = lax.rem(line, 2), lax.rem(z, 2)
     group = up * 2 + right
 
@@ -175,6 +175,12 @@
     def row(i):
         return lax.rem(line + i, NK)
 
+    def near(i):
+        back = line >= 2
+        me = jnp.where(back, NK - 1 - line, line)
+        k = i - 1 + (i - 1 >= me).astype(jnp.int32)
+        return jnp.where(back, NK - 1 - k, k)
+
     def part(i):
         return pl.ds(pl.multiple_of(i * rows, 16), rows)
 
@@ -202,7 +208,7 @@
         first = y - line
 
         def send(i, carry):
-            k = row(i + 1)
+            k = i
 
             def place_z(j):
                 zt = column(j, 0)
@@ -228,20 +234,12 @@
                 send_y(i, 0)
 
     def scatter0_end():
-        first = y - line
-
-        def add_z(i):
-            k = row(i + 1)
+        def add_z(k):
             arrived(landz.at[k], az_recv.at[k])
             midz[k] = total(landz.at[k])
-
-            @pl.when(k == line)
-            def _():
-                pltpu.make_async_copy(midz.at[k], finy.at[line], by_recv).start()
-
-            @pl.when(k != line)
-            def _():
-                remote(midz.at[k], finy.at[line], by_send, by_recv, seq_at(first + k, z)).start()
+            pltpu.make_async_copy(midz.at[k], landp.at[k, line], p_recv.at[k]).start()
+            for i in range(NK):
+                remote(midz.at[k], landp.at[k, line], p_send.at[0], p_recv.at[k], seq_at(NK + row(i + 2), z)).start()
 
         def add_y(i):
             zt = column(i, 1)
@@ -266,11 +264,6 @@
                 def _():
                     add_z(i)
 
-        @pl.when(y_first)
-        def _():
-            arrived(finy, by_recv)
-            g_all0[line, part(z), :] = total(finy)
-
         @pl.when(jnp.logical_not(y_first))
         def _():
             arrived(finz, bz_recv)
@@ -285,8 +278,8 @@
         lax.fori_loop(0, nz - 1, one, 0)
 
     def to_own_span(block, send, recv):
-        for i in range(1, NK):
-            remote(block, block, send, recv, seq_at(y - line + row(i), z)).start()
+        for i in range(NK - 1, 0, -1):
+            remote(block, block, send, recv, seq_at(y - line + near(i), z)).start()
 
     def to_span1(block, send, recv):
         for i in range(NK):
@@ -297,7 +290,7 @@
             return g_all0.at[k, part(zt)]
 
         def column0(i):
-            return 4 * lax.rem(z // 4 + i, fourth) + 3 - 2 * c
+            return 4 * lax.rem(z // 4 + i, fourth) + 3 - c
 
         own = block(line, z)
 
@@ -305,9 +298,16 @@
             arrived(block(k, z), y_recv.at[0, k])
             to_z(block(k, z), z_send.at[0], z_recv.at[0])
 
+        def add_rows(k):
+            arrived(landp.at[k], p_recv.at[k])
+            g_all0[k, part(z), :] = total(landp.at[k])
+            to_z(block(k, z), z_send.at[0], z_recv.at[0])
+
+        owner_y = y_first0 & jnp.logical_not(y_first)
+
         @pl.when(span == 0)
         def _():
-            @pl.when(y_first0)
+            @pl.when(owner_y)
             def _():
                 to_span1(own, y_send.at[0], y_recv.at[0, line])
                 to_own_span(own, y_send.at[1], y_recv.at[0, line])
@@ -328,16 +328,27 @@
             for i in range(fourth):
                 to_own_span(block(line, column0(i)), fy_send.at[1], fy_recv.at[0])
 
-            @pl.when(y_first0)
+            @pl.when(y_first)
+            def _():
+                for k in range(NK):
+                    for i in range(1, NK):
+                        remote(midz.at[k], landp.at[k, line], p_send.at[1], p_recv.at[k], seq_at(row(i), z)).start()
+
+            @pl.when(owner_y)
             def _():
                 to_z(own, z_send.at[0], z_recv.at[0])
                 for i in range(1, NK):
                     forward_z(row(i))
 
-        @pl.when((span == 1) & y_first0)
+        @pl.when((span == 1) & owner_y)
         def _():
             for i in range(NK):
                 forward_z(jnp.where(line >= 2, i, NK - 1 - i))
+
+        @pl.when(y_first)
+        def _():
+            for k in range(NK):
+                add_rows(k)
 
     def gathered(p, along_y_first, columns):
         @pl.when(along_y_first)
@@ -377,7 +388,7 @@
 
                 @pl.when(y_first)
                 def _():
-                    k = row(i)
+                    k = near(i)
                     arrived(place1(k, z), y_recv.at[1, k])
                     to_z(place1(k, z), z_send.at[1], z_recv.at[1])
 
@@ -586,9 +597,10 @@
 
         @pl.when(y_first)
         def _():
-            arrived(three, by_send)
-
-        @pl.when(y_first0)
+            arrived(landp, p_send.at[0])
+            arrived(landp.at[:, pl.ds(0, NK - 1)], p_send.at[1])
+
+        @pl.when(y_first0 & z_first)
         def _():
             arrived(finy, y_send.at[0])
             arrived(three, y_send.at[1])
@@ -644,6 +656,7 @@
             pltpu.VMEM(full, BF16),
             pltpu.VMEM((NK, nz, rows, LANES), BF16),
             pltpu.VMEM((NK, rows, LANES), BF16),
+            pltpu.VMEM((NK, NK, rows, LANES), BF16),
             pltpu.VMEM((NK, rows, LANES), BF16),
             pltpu.VMEM((nz // 2, NK, rows, LANES), BF16),
             pltpu.VMEM((nz // 2, rows, LANES), BF16),
@@ -671,8 +684,8 @@
             dma((nz // 2,)),
             dma,
             dma,
-            dma,
-            dma,
+            dma((2,)),
+            dma((NK,)),
             dma,
             dma,
             dma((2,)),

time: 63.1 us -> 60.3 us (0.956)
  the two profiles are of different devices: /device:TPU:51 before, /device:TPU:63 now
where the time goes in v6:
time: 60.3 us; the launch traced here: 60.1 us
  Pallas kernels  58.5 us (97%)
  local copies, waits for them, and re-layouts  1.57 us (3%)
    pallas_call x1, Pallas kernels, local(): pl.pallas_call(functools.partial(kernel, ny, nz), out_shape=jax.ShapeDtyp...  58.5 us
    unnamed x1, local copies, waits for them, and re-layouts  1.57 us

profile of v6, /device:TPU:63, one launch (start us, length us, event | category | flops | bytes accessed | tf_op | source)
XLA Modules:
  0.0 60.1 jit_solution(5456748834985651612)
XLA Ops:
  0.0 58.5 %fast_layer.1 = bf16[128,512]{1,0:T(8,128)(2,1)} custom-call(bf16[128,512]{1,0:T(8,128)(2,1)} %q_hbm.1, bf16[128,512]{1,0:T(8,128)(2,1)} %k_hbm.1, bf16[128,512]{1,0:T(8,128)(2,1)} %v_hbm.1, f32[1,128]{1,0:T(1,128)} %bitcast.1, bf16[1,512,256]{2,1,0:T(8,128)(2,1)} %wg_hbm.1, bf16[1,512,256]{2,1,0:T(8,128)(2,1)} %wu_hbm.1, bf16[1,512,256]{2,1,0:T(8,128)(2,1)} %wd_hbm.1), custom_call_target="tpu_custom_call" | custom-call | tf_op jit(solution)/shard_map/fast_layer/pallas_call | solution.py:634
  58.5 1.6 %copy.9 = bf16[128,512]{1,0:T(8,128)(2,1)} copy(bf16[128,512]{1,0:T(8,128)(2,1)} %fast_layer.1) | data formatting | bytes 262144

commit v7 on v6

--- a/solution.py
+++ b/solution.py
@@ -376,14 +376,6 @@
             to_own_span(own, fy_send.at[0], fy_recv.at[1])
 
         for i in range(max(NK, half)):
-            if i < half:
-                zt = column(half - 1 - i, 1)
-
-                @pl.when(zt != z)
-                def _():
-                    arrived(place1(line, zt), zy_recv.at[1, zt])
-                    to_own_span(place1(line, zt), fy_send.at[0], fy_recv.at[1])
-
             if 1 <= i < NK:
 
                 @pl.when(y_first)
@@ -391,6 +383,14 @@
                     k = near(i)
                     arrived(place1(k, z), y_recv.at[1, k])
                     to_z(place1(k, z), z_send.at[1], z_recv.at[1])
+
+            if i < half:
+                zt = column(half - 1 - i, 1)
+
+                @pl.when(zt != z)
+                def _():
+                    arrived(place1(line, zt), zy_recv.at[1, zt])
+                    to_own_span(place1(line, zt), fy_send.at[0], fy_recv.at[1])
 
     def initial_weights():
         first = pl.multiple_of(c * HALF, HALF)
@@ -702,7 +702,7 @@
             dma,
         ],
         compiler_params=pltpu.CompilerParams(
-            collective_id=0, has_side_effects=True, vmem_limit_bytes=60 * 2**20
+            collective_id=0, has_side_effects=True, vmem_limit_bytes=55040 * 1024
         ),
         name="fast_layer",
     )(queries, keys, values, rates.reshape(1, T), gate_fast, up_fast, down_fast)

time: 60.3 us -> 59.4 us (0.985)
    pallas_call x1, Pallas kernels: 58.5 us -> 57.9 us  [local(): pl.pallas_call(functools.partial(kernel, ny, nz), out_shape=jax.ShapeDtyp...]
    unnamed x1 -> x3, local copies, waits for them, and re-layouts: 1.57 us -> 1.31 us
where the time goes in v7:
time: 59.4 us; the launch traced here: 59.2 us
  Pallas kernels  57.9 us (97%)
  local copies, waits for them, and re-layouts  1.31 us (2%)
    pallas_call x1, Pallas kernels, local(): pl.pallas_call(functools.partial(kernel, ny, nz), out_shape=jax.ShapeDtyp...  57.9 us
    unnamed x3, local copies, waits for them, and re-layouts  1.31 us

profile of v7, /device:TPU:63, one launch (start us, length us, event | category | flops | bytes accessed | tf_op | source)
XLA Modules:
  0.0 59.2 jit_solution(4450380212011819436)
XLA Ops:
  0.0 0.0 copy-start
  0.0 0.7 %copy-done = f32[128,1]{0,1:T(1,128)S(1)} copy-done((f32[128,1]{0,1:T(1,128)S(1)}, f32[128,1]{0,1:T(1,128)}, u32[]{:S(2)}) %copy-start) | copy-done | bytes 536
  0.7 57.9 %fast_layer.1 = bf16[128,512]{1,0:T(8,128)(2,1)S(1)} custom-call(bf16[128,512]{1,0:T(8,128)(2,1)} %q_hbm.1, bf16[128,512]{1,0:T(8,128)(2,1)} %k_hbm.1, bf16[128,512]{1,0:T(8,128)(2,1)} %v_hbm.1, f32[1,128]{1,0:T(1,128)S(1)} %bitcast.1, bf16[1,512,256]{2,1,0:T(8,128)(2,1)} %wg_hbm.1, bf16[1,512,256]{2,1,0:T(8,128)(2,1)} %wu_hbm.1, bf16[1,512,256]{2,1,0:T(8,128)(2,1)} %wd_hbm.1), custom_call_target="tpu_custom_call" | custom-call | tf_op jit(solution)/shard_map/fast_layer/pallas_call | solution.py:634
  58.6 0.7 %copy.9 = bf16[128,512]{1,0:T(8,128)(2,1)} copy(bf16[128,512]{1,0:T(8,128)(2,1)S(1)} %fast_layer.1) | data formatting | bytes 262144
Async XLA Ops:
  0.0 0.7 %copy-start = (f32[128,1]{0,1:T(1,128)S(1)}, f32[128,1]{0,1:T(1,128)}, u32[]{:S(2)}) copy-start(f32[128,1]{0,1:T(1,128)} %param.10) | copy-start | bytes 1540

commit v8 on v7

--- a/solution.py
+++ b/solution.py
@@ -193,7 +193,7 @@
             out = out + ref[i].astype(F32)
         return out.astype(BF16)
 
-    give = remote(g_give, g_got, gh_send, gh_recv, partner)
+    gives = [remote(g_give.at[k], g_got.at[k], gh_send.at[k], gh_recv.at[k], partner) for k in range(NK)]
     shares = [
         remote(ref, ref, x_send.at[i], x_recv.at[i], partner)
         for i, ref in enumerate((kk.at[group, c], vv.at[group, c], rr.at[group, c], qq.at[c]))
@@ -433,12 +433,14 @@
 
     @pl.when(span == 0)
     def _():
-        give.start()
+        for give in gives:
+            give.start()
         for share in shares:
             share.start()
         pl.when((c == 1) & last_chip)(start_halo)
-        give.wait_recv()
-        g_send0[...] = (g_own[...] + g_got[...].astype(F32)).astype(BF16)
+        for k, give in enumerate(gives):
+            give.wait_recv()
+            g_send0[k] = (g_own[k] + g_got[k].astype(F32)).astype(BF16)
         scatter0()
         initial_weights()
         for share in shares:
@@ -551,12 +553,12 @@
             w_high, w_low = w_b[0, 2 * HALF:3 * HALF], w_b[1, 2 * HALF:3 * HALF]
             return dot_nn(high, w_high) + (dot_nn(low, w_high) + dot_nn(high, w_low))
 
-        f_give[...] = half_sum(qq[1 - c])
+        f_give[...] = half_sum(qq[1 - c]).astype(BF16)
         swap = remote(f_give, f_got, f_send, f_recv, partner)
         swap.start()
         mine = half_sum(qq[c])
         swap.wait()
-        f = mine + f_got[...]
+        f = mine + f_got[...].astype(F32)
         fast = (f * lax.rsqrt(jnp.mean(f * f, axis=1, keepdims=True) + 1e-06)).astype(BF16)
         out_ref[...] = (attn[...] + fast.astype(F32)).astype(BF16)
 
@@ -588,7 +590,8 @@
 
     @pl.when(span == 0)
     def _():
-        give.wait_send()
+        for give in gives:
+            give.wait_send()
         left(lambda n: landz.at[:, pl.ds(0, half - n)], az_send, y_first)
         arrived(landy.at[:, pl.ds(0, NK - 1)], ay_send)
         left(lambda n: finz.at[pl.ds(0, half - n)], bz_send, z_first)
@@ -665,15 +668,15 @@
             pltpu.VMEM((2, 16, LANES), F32),
             pltpu.VMEM((2, 16, LANES), F32),
             pltpu.VMEM((T, DH), F32),
-            pltpu.VMEM((T, DH), F32),
-            pltpu.VMEM((T, DH), F32),
+            pltpu.VMEM((T, DH), BF16),
+            pltpu.VMEM((T, DH), BF16),
             dma((7,)),
             dma((4,)),
             dma((4,)),
             dma((2,)),
             dma((2,)),
-            dma,
-            dma,
+            dma((NK,)),
+            dma((NK,)),
             dma((3,)),
             dma((3, NK)),
             dma((3,)),

time: 59.4 us -> 58.9 us (level)
  no operation moved by 1% of the time
where the time goes in v8:
time: 58.9 us; the launch traced here: 58.7 us
  Pallas kernels  57.4 us (97%)
  local copies, waits for them, and re-layouts  1.31 us (2%)
    pallas_call x1, Pallas kernels, local(): pl.pallas_call(functools.partial(kernel, ny, nz), out_shape=jax.ShapeDtyp...  57.4 us
    unnamed x3, local copies, waits for them, and re-layouts  1.31 us

profile of v8, /device:TPU:63, one launch (start us, length us, event | category | flops | bytes accessed | tf_op | source)
XLA Modules:
  0.0 58.7 jit_solution(3259872911044900425)
XLA Ops:
  0.0 0.0 copy-start
  0.0 0.7 %copy-done = f32[128,1]{0,1:T(1,128)S(1)} copy-done((f32[128,1]{0,1:T(1,128)S(1)}, f32[128,1]{0,1:T(1,128)}, u32[]{:S(2)}) %copy-start) | copy-done | bytes 536
  0.7 57.4 %fast_layer.1 = bf16[128,512]{1,0:T(8,128)(2,1)S(1)} custom-call(bf16[128,512]{1,0:T(8,128)(2,1)} %q_hbm.1, bf16[128,512]{1,0:T(8,128)(2,1)} %k_hbm.1, bf16[128,512]{1,0:T(8,128)(2,1)} %v_hbm.1, f32[1,128]{1,0:T(1,128)S(1)} %bitcast.1, bf16[1,512,256]{2,1,0:T(8,128)(2,1)} %wg_hbm.1, bf16[1,512,256]{2,1,0:T(8,128)(2,1)} %wu_hbm.1, bf16[1,512,256]{2,1,0:T(8,128)(2,1)} %wd_hbm.1), custom_call_target="tpu_custom_call" | custom-call | tf_op jit(solution)/shard_map/fast_layer/pallas_call | solution.py:637
  58.1 0.7 %copy.9 = bf16[128,512]{1,0:T(8,128)(2,1)} copy(bf16[128,512]{1,0:T(8,128)(2,1)S(1)} %fast_layer.1) | data formatting | bytes 262144
Async XLA Ops:
  0.0 0.7 %copy-start = (f32[128,1]{0,1:T(1,128)S(1)}, f32[128,1]{0,1:T(1,128)}, u32[]{:S(2)}) copy-start(f32[128,1]{0,1:T(1,128)} %param.10) | copy-start | bytes 1540

commit v9 on v8

--- a/solution.py
+++ b/solution.py
@@ -175,6 +175,9 @@
     def row(i):
         return lax.rem(line + i, NK)
 
+    def across(i):
+        return jnp.where(line < 2, i, NK - 1 - i)
+
     def near(i):
         back = line >= 2
         me = jnp.where(back, NK - 1 - line, line)
@@ -239,7 +242,7 @@
             midz[k] = total(landz.at[k])
             pltpu.make_async_copy(midz.at[k], landp.at[k, line], p_recv.at[k]).start()
             for i in range(NK):
-                remote(midz.at[k], landp.at[k, line], p_send.at[0], p_recv.at[k], seq_at(NK + row(i + 2), z)).start()
+                remote(midz.at[k], landp.at[k, line], p_send.at[0], p_recv.at[k], seq_at(NK + across(i), z)).start()
 
         def add_y(i):
             zt = column(i, 1)
@@ -283,7 +286,7 @@
 
     def to_span1(block, send, recv):
         for i in range(NK):
-            remote(block, block, send, recv, seq_at(NK + row(i + 2), z)).start()
+            remote(block, block, send, recv, seq_at(NK + across(i), z)).start()
 
     def gather0():
         def block(k, zt):

time: 58.9 us -> 58.8 us (level)
  the two profiles are of different devices: /device:TPU:63 before, /device:TPU:61 now
where the time goes in v9:
time: 58.8 us; the launch traced here: 58.7 us
  Pallas kernels  57.3 us (97%)
  local copies, waits for them, and re-layouts  1.31 us (2%)
    pallas_call x1, Pallas kernels, local(): pl.pallas_call(functools.partial(kernel, ny, nz), out_shape=jax.ShapeDtyp...  57.3 us
    unnamed x3, local copies, waits for them, and re-layouts  1.31 us

profile of v9, /device:TPU:61, one launch (start us, length us, event | category | flops | bytes accessed | tf_op | source)
XLA Modules:
  0.0 58.7 jit_solution(16076965916370196606)
XLA Ops:
  0.0 0.0 copy-start
  0.0 0.7 %copy-done = f32[128,1]{0,1:T(1,128)S(1)} copy-done((f32[128,1]{0,1:T(1,128)S(1)}, f32[128,1]{0,1:T(1,128)}, u32[]{:S(2)}) %copy-start) | copy-done | bytes 536
  0.7 57.3 %fast_layer.1 = bf16[128,512]{1,0:T(8,128)(2,1)S(1)} custom-call(bf16[128,512]{1,0:T(8,128)(2,1)} %q_hbm.1, bf16[128,512]{1,0:T(8,128)(2,1)} %k_hbm.1, bf16[128,512]{1,0:T(8,128)(2,1)} %v_hbm.1, f32[1,128]{1,0:T(1,128)S(1)} %bitcast.1, bf16[1,512,256]{2,1,0:T(8,128)(2,1)} %wg_hbm.1, bf16[1,512,256]{2,1,0:T(8,128)(2,1)} %wu_hbm.1, bf16[1,512,256]{2,1,0:T(8,128)(2,1)} %wd_hbm.1), custom_call_target="tpu_custom_call" | custom-call | tf_op jit(solution)/shard_map/fast_layer/pallas_call | solution.py:640
  58.0 0.7 %copy.9 = bf16[128,512]{1,0:T(8,128)(2,1)} copy(bf16[128,512]{1,0:T(8,128)(2,1)S(1)} %fast_layer.1) | data formatting | bytes 262144
Async XLA Ops:
  0.0 0.7 %copy-start = (f32[128,1]{0,1:T(1,128)S(1)}, f32[128,1]{0,1:T(1,128)}, u32[]{:S(2)}) copy-start(f32[128,1]{0,1:T(1,128)} %param.10) | copy-start | bytes 1540

commit v10 on v9

--- a/solution.py
+++ b/solution.py
@@ -224,7 +224,7 @@
             zt = column(i, 1)
 
             def place_y(j):
-                k = row(j + 1)
+                k = jnp.where(j == NK - 1, line, near(NK - 1 - j))
                 return k, seq_at(first + k, z)
 
             fan(NK, place_y, lambda k: g_send0.at[k, part(zt)], lambda k: landy.at[zt // 2, line], ay_send, ay_recv.at[zt // 2])

time: 58.8 us -> 58.5 us (level)
  the two profiles are of different devices: /device:TPU:61 before, /device:TPU:63 now
where the time goes in v10:
time: 58.5 us; the launch traced here: 58.4 us
  Pallas kernels  57 us (97%)
  local copies, waits for them, and re-layouts  1.31 us (2%)
    pallas_call x1, Pallas kernels, local(): pl.pallas_call(functools.partial(kernel, ny, nz), out_shape=jax.ShapeDtyp...  57 us
    unnamed x3, local copies, waits for them, and re-layouts  1.31 us

profile of v10, /device:TPU:63, one launch (start us, length us, event | category | flops | bytes accessed | tf_op | source)
XLA Modules:
  0.0 58.4 jit_solution(7921695686003264795)
XLA Ops:
  0.0 0.0 copy-start
  0.0 0.7 %copy-done = f32[128,1]{0,1:T(1,128)S(1)} copy-done((f32[128,1]{0,1:T(1,128)S(1)}, f32[128,1]{0,1:T(1,128)}, u32[]{:S(2)}) %copy-start) | copy-done | bytes 536
  0.7 57.0 %fast_layer.1 = bf16[128,512]{1,0:T(8,128)(2,1)S(1)} custom-call(bf16[128,512]{1,0:T(8,128)(2,1)} %q_hbm.1, bf16[128,512]{1,0:T(8,128)(2,1)} %k_hbm.1, bf16[128,512]{1,0:T(8,128)(2,1)} %v_hbm.1, f32[1,128]{1,0:T(1,128)S(1)} %bitcast.1, bf16[1,512,256]{2,1,0:T(8,128)(2,1)} %wg_hbm.1, bf16[1,512,256]{2,1,0:T(8,128)(2,1)} %wu_hbm.1, bf16[1,512,256]{2,1,0:T(8,128)(2,1)} %wd_hbm.1), custom_call_target="tpu_custom_call" | custom-call | tf_op jit(solution)/shard_map/fast_layer/pallas_call | solution.py:640
  57.7 0.7 %copy.9 = bf16[128,512]{1,0:T(8,128)(2,1)} copy(bf16[128,512]{1,0:T(8,128)(2,1)S(1)} %fast_layer.1) | data formatting | bytes 262144
Async XLA Ops:
  0.0 0.7 %copy-start = (f32[128,1]{0,1:T(1,128)S(1)}, f32[128,1]{0,1:T(1,128)}, u32[]{:S(2)}) copy-start(f32[128,1]{0,1:T(1,128)} %param.10) | copy-start | bytes 1540
